TPU v7x, 32 devices: a whole 2x2x4 slice. The times are simulated.
32 devices in a mesh: outer: 4 (over x, core), dp: 8 (over z, y).
Axes of the slice: x: 2, y: 2, z: 4, core: 2. Of those that a mesh axis runs over, the one named last changes fastest.
Arguments:
- query_ids: int32 [32, 512], P(('outer', 'dp')), may hold values from 0 to 30521
- query_mask: int32 [32, 512], P(('outer', 'dp')), may hold values from 0 to 1, as said below
- passage_ids: int32 [32, 512], P(('outer', 'dp')), may hold values from 0 to 30521
- passage_mask: int32 [32, 512], P(('outer', 'dp')), may hold values from 0 to 1, as said below
- source: int32 [32], replicated, may hold values from 0 to 3
- positive: int32 [32], replicated, may hold values from 0 to 31, each once
- table: float32 [30720, 768], P(('outer', 'dp')), may hold values from -0.3125 to 0.3125
- positions: float32 [512, 768], P(('outer', 'dp')), may hold values from -0.3125 to 0.3125
- w_qkv: float32 [768, 2304], P(('outer', 'dp')), may hold values from -0.21875 to 0.21875
- w_o: float32 [768, 768], P(('outer', 'dp')), may hold values from -0.875 to 0.875
- w_in: float32 [768, 3072], P(('outer', 'dp')), may hold values from -0.21875 to 0.21875
- w_out: float32 [3072, 768], P(('outer', 'dp')), may hold values from -0.109375 to 0.109375
- vectors: float32 [14, 768], P(None, ('outer', 'dp')), may hold values from -0.4 to 1.4, as said below
- first_table: float32 [30720, 768], P(('outer', 'dp')), may hold values from -5.722046e-06 to 5.722046e-06
- first_positions: float32 [512, 768], P(('outer', 'dp')), may hold values from -5.722046e-06 to 5.722046e-06
- first_qkv: float32 [768, 2304], P(('outer', 'dp')), may hold values from -5.722046e-06 to 5.722046e-06
- first_o: float32 [768, 768], P(('outer', 'dp')), may hold values from -5.722046e-06 to 5.722046e-06
- first_in: float32 [768, 3072], P(('outer', 'dp')), may hold values from -5.722046e-06 to 5.722046e-06
- first_out: float32 [3072, 768], P(('outer', 'dp')), may hold values from -5.722046e-06 to 5.722046e-06
- first_vectors: float32 [14, 768], P(None, ('outer', 'dp')), may hold values from -3.0517578e-05 to 3.0517578e-05
- second_table: float32 [30720, 768], P(('outer', 'dp')), may hold values from 1.60902e-12 to 6.43608e-12
- second_positions: float32 [512, 768], P(('outer', 'dp')), may hold values from 8.0451e-14 to 3.21804e-13
- second_qkv: float32 [768, 2304], P(('outer', 'dp')), may hold values from 8.0451e-14 to 3.21804e-13
- second_o: float32 [768, 768], P(('outer', 'dp')), may hold values from 8.0451e-14 to 3.21804e-13
- second_in: float32 [768, 3072], P(('outer', 'dp')), may hold values from 8.0451e-14 to 3.21804e-13
- second_out: float32 [3072, 768], P(('outer', 'dp')), may hold values from 8.0451e-14 to 3.21804e-13
- second_vectors: float32 [14, 768], P(None, ('outer', 'dp')), may hold values from 2.011275e-12 to 8.0451e-12
Outputs:
- new_table: float32 [30720, 768], P(('outer', 'dp'))
- new_positions: float32 [512, 768], P(('outer', 'dp'))
- new_qkv: float32 [768, 2304], P(('outer', 'dp'))
- new_o: float32 [768, 768], P(('outer', 'dp'))
- new_in: float32 [768, 3072], P(('outer', 'dp'))
- new_out: float32 [3072, 768], P(('outer', 'dp'))
- new_vectors: float32 [14, 768], P(None, ('outer', 'dp'))
- moment_table: float32 [30720, 768], P(('outer', 'dp'))
- moment_positions: float32 [512, 768], P(('outer', 'dp'))
- moment_qkv: float32 [768, 2304], P(('outer', 'dp'))
- moment_o: float32 [768, 768], P(('outer', 'dp'))
- moment_in: float32 [768, 3072], P(('outer', 'dp'))
- moment_out: float32 [3072, 768], P(('outer', 'dp'))
- moment_vectors: float32 [14, 768], P(None, ('outer', 'dp'))
- square_table: float32 [30720, 768], P(('outer', 'dp'))
- square_positions: float32 [512, 768], P(('outer', 'dp'))
- square_qkv: float32 [768, 2304], P(('outer', 'dp'))
- square_o: float32 [768, 768], P(('outer', 'dp'))
- square_in: float32 [768, 3072], P(('outer', 'dp'))
- square_out: float32 [3072, 768], P(('outer', 'dp'))
- square_vectors: float32 [14, 768], P(None, ('outer', 'dp'))
- loss: float32 [], replicated
- grad_norm: float32 [], replicated
Inputs may be any that keep to these rules, and one draw needn't show every extreme that they name: `query_mask`: each row is 1 on a prefix of 64 or more positions and 0 after it. `passage_mask`: each row is 1 on a prefix of 128 or more positions and 0 after it. `vectors`: rows 8, 10, 12 lie within 0.6 to 1.4, the others within -0.4 to 0.4.
All inputs are finite; a program needn't handle non-finite values.
Results may differ from a plain program's by a relative error of at most 0.012.
The roundings to bfloat16 on the way count: a program that leaves them out, or rounds other values in their place, can miss the bound.
Values may be sent and summed in bfloat16 or wider, within the bound.
No kernel may reach another device: no remote copies, remote signals or barrier semaphores. Data moves between devices by JAX's collectives and lax.ppermute only.
A program may use at most 320 MiB of HBM per device.

v0:
```python
import jax
import jax.numpy as jnp
from jax import lax
from jax.sharding import PartitionSpec as P

D = 768
HEADS = 12
HEAD_DIM = 64
M1 = 64
M2 = 128
M3 = 256
STEP = 10


TEMPER = 0.01
CLIP_LIMIT = 0.05
LEARN_RATE = 0.1
VECTOR_RATE = 0.3
BETA_FIRST = 0.9
BETA_SECOND = 0.999
WEIGHT_DECAY = 0.01
EPSILON = 1e-08
NORM_EPSILON = 1e-12
PRECISE = lax.Precision.HIGHEST


def layer_norm(values, gain_row, shift_row):
    centre = values - jnp.mean(values, -1, keepdims=True)
    spread = jnp.mean(centre * centre, -1, keepdims=True)
    return centre * lax.rsqrt(spread + NORM_EPSILON) * gain_row + shift_row


def gelu_exact(values):
    return jax.nn.gelu(values, approximate=False)


def matmul(left, right):
    return jnp.dot(left, right, preferred_element_type=jnp.float32)


def pool(hidden_two, token_mask):
    weight_mask = token_mask.astype(jnp.float32)
    pooled = jnp.sum(hidden_two * weight_mask[:, :, None], 1) / jnp.sum(weight_mask, 1)[:, None]
    return pooled * lax.rsqrt(jnp.sum(pooled * pooled, -1, keepdims=True) + NORM_EPSILON)


def attention_scores(packed, token_mask):
    scores = jnp.einsum(
        "sqhc,skhc->shqk", packed[:, :, 0], packed[:, :, 1], preferred_element_type=jnp.float32
    ) * HEAD_DIM ** (-0.5)
    return jnp.where(token_mask[:, None, None, :] > 0, scores, -1000000000.0)


def forward(matrices, vector_rows, embedded, token_mask):
    qkv_w, proj_w, inner_w, outer_w = matrices
    sequences, length, model_width = embedded.shape
    hidden_zero = layer_norm(embedded, vector_rows[8], vector_rows[9]).reshape(-1, model_width)
    bias_qkv = jnp.concatenate([vector_rows[0], jnp.zeros_like(vector_rows[0]), vector_rows[1]])
    packed = (matmul(hidden_zero.astype(jnp.bfloat16), qkv_w) + bias_qkv).astype(jnp.bfloat16)
    packed = packed.reshape(sequences, length, 3, HEADS, HEAD_DIM)
    scores = attention_scores(packed, token_mask)
    row_peak = jnp.max(scores, -1, keepdims=True)
    exponent = jnp.exp(scores - row_peak)
    row_total = jnp.sum(exponent, -1, keepdims=True)
    log_total = row_peak + jnp.log(row_total)
    attn_weights = (exponent / row_total).astype(jnp.bfloat16)
    context = jnp.einsum(
        "shqk,skhc->sqhc", attn_weights, packed[:, :, 2], preferred_element_type=jnp.float32
    )
    context = context.astype(jnp.bfloat16).reshape(-1, model_width)
    mixed_one = hidden_zero + matmul(context, proj_w) + vector_rows[2]
    hidden_one = layer_norm(mixed_one, vector_rows[10], vector_rows[11])
    inner_pre = matmul(hidden_one.astype(jnp.bfloat16), inner_w) + vector_rows[3:7].reshape(-1)
    activated = gelu_exact(inner_pre).astype(jnp.bfloat16)
    mixed_two = hidden_one + matmul(activated, outer_w) + vector_rows[7]
    hidden_two = layer_norm(mixed_two, vector_rows[12], vector_rows[13]).reshape(
        sequences, length, model_width
    )
    saved_state = (
        hidden_zero,
        packed,
        log_total,
        context,
        mixed_one,
        inner_pre,
        activated,
        mixed_two,
    )
    return (hidden_two, saved_state)


def backward(matrices, vector_rows, embedded, token_mask, saved_state, grad_hidden):
    qkv_w, proj_w, inner_w, outer_w = matrices
    hidden_zero, packed, log_total, context, mixed_one, inner_pre, activated, mixed_two = (
        saved_state
    )
    sequences, length, model_width = embedded.shape
    _, norm_two_back = jax.vjp(layer_norm, mixed_two, vector_rows[12], vector_rows[13])
    grad_two, grad_gain_two, grad_shift_two = norm_two_back(grad_hidden.reshape(-1, model_width))
    hidden_one, norm_one_back = jax.vjp(layer_norm, mixed_one, vector_rows[10], vector_rows[11])
    grad_branch = grad_two.astype(jnp.bfloat16)
    grad_outer_w = matmul(activated.T, grad_branch)
    grad_outer_b = jnp.sum(grad_branch.astype(jnp.float32), 0)
    _, gelu_back = jax.vjp(gelu_exact, inner_pre)
    grad_inner = gelu_back(matmul(grad_branch, outer_w.T))[0].astype(jnp.bfloat16)
    grad_inner_w = matmul(hidden_one.astype(jnp.bfloat16).T, grad_inner)
    grad_inner_b = jnp.sum(grad_inner.astype(jnp.float32), 0)
    grad_one = grad_two + matmul(grad_inner, inner_w.T)
    grad_mixed, grad_gain_one, grad_shift_one = norm_one_back(grad_one)
    grad_attended = grad_mixed.astype(jnp.bfloat16)
    grad_proj_w = matmul(context.T, grad_attended)
    grad_proj_b = jnp.sum(grad_attended.astype(jnp.float32), 0)
    grad_context = matmul(grad_attended, proj_w.T).astype(jnp.bfloat16)
    grad_context = grad_context.reshape(sequences, length, HEADS, HEAD_DIM)
    scores = attention_scores(packed, token_mask)
    attn_weights = jnp.exp(scores - log_total)
    grad_values = jnp.einsum(
        "shqk,sqhc->skhc",
        attn_weights.astype(jnp.bfloat16),
        grad_context,
        preferred_element_type=jnp.float32,
    )
    grad_weights = jnp.einsum(
        "sqhc,skhc->shqk", grad_context, packed[:, :, 2], preferred_element_type=jnp.float32
    )
    grad_scores = attn_weights * (
        grad_weights - jnp.sum(grad_weights * attn_weights, -1, keepdims=True)
    )
    grad_scores = grad_scores.astype(jnp.bfloat16)
    grad_queries = jnp.einsum(
        "shqk,skhc->sqhc", grad_scores, packed[:, :, 1], preferred_element_type=jnp.float32
    ) * HEAD_DIM ** (-0.5)
    grad_keys = jnp.einsum(
        "shqk,sqhc->skhc", grad_scores, packed[:, :, 0], preferred_element_type=jnp.float32
    ) * HEAD_DIM ** (-0.5)
    grad_packed = jnp.stack([grad_queries, grad_keys, grad_values], 2).astype(jnp.bfloat16)
    grad_packed = grad_packed.reshape(-1, 3 * model_width)
    grad_qkv_w = matmul(hidden_zero.astype(jnp.bfloat16).T, grad_packed)
    packed_sums = jnp.sum(grad_packed.astype(jnp.float32), 0)
    grad_zero = matmul(grad_packed, qkv_w.T) + grad_mixed
    _, norm_zero_back = jax.vjp(
        layer_norm, embedded.reshape(-1, model_width), vector_rows[8], vector_rows[9]
    )
    grad_input, grad_gain_zero, grad_shift_zero = norm_zero_back(grad_zero)
    grad_vectors = jnp.concatenate(
        [
            jnp.stack([packed_sums[:model_width], packed_sums[2 * model_width :], grad_proj_b]),
            grad_inner_b.reshape(4, model_width),
            jnp.stack(
                [
                    grad_outer_b,
                    grad_gain_zero,
                    grad_shift_zero,
                    grad_gain_one,
                    grad_shift_one,
                    grad_gain_two,
                    grad_shift_two,
                ]
            ),
        ]
    )
    grad_matrices = (grad_qkv_w, grad_proj_w, grad_inner_w, grad_outer_w)
    return (grad_input.reshape(sequences, length, model_width), grad_matrices, grad_vectors)


def info_loss(queries, passages, query_rows, source, positive):
    own_positive = jnp.take(positive, query_rows)
    keeping = source[None, :] == jnp.take(source, own_positive)[:, None]
    total = jnp.zeros((), jnp.float32)
    for nested in (M1, M2, M3, D):
        left = queries[:, :nested]
        left = left * lax.rsqrt(jnp.sum(left * left, -1, keepdims=True) + NORM_EPSILON)
        right = passages[:, :nested]
        right = right * lax.rsqrt(jnp.sum(right * right, -1, keepdims=True) + NORM_EPSILON)
        scores = jnp.dot(left, right.T, precision=PRECISE) / TEMPER
        scores = jnp.where(keeping, scores, -1000000000.0)
        row_peak = jnp.max(scores, -1, keepdims=True)
        log_total = row_peak[:, 0] + jnp.log(jnp.sum(jnp.exp(scores - row_peak), -1))
        target = jnp.take_along_axis(scores, own_positive[:, None], 1)[:, 0]
        total = total + jnp.sum(log_total - target)
    return total / passages.shape[0]


def per_device(
    query_ids,
    query_mask,
    passage_ids,
    passage_mask,
    source,
    positive,
    table,
    positions,
    w_qkv,
    w_o,
    w_in,
    w_out,
    vectors,
    first_table,
    first_positions,
    first_qkv,
    first_o,
    first_in,
    first_out,
    first_vectors,
    second_table,
    second_positions,
    second_qkv,
    second_o,
    second_in,
    second_out,
    second_vectors,
):
    gathered = (
        lax.all_gather(table.astype(jnp.bfloat16), ("outer", "dp"), axis=0, tiled=True),
        lax.all_gather(positions.astype(jnp.bfloat16), ("outer", "dp"), axis=0, tiled=True),
        lax.all_gather(w_qkv.astype(jnp.bfloat16), ("outer", "dp"), axis=0, tiled=True),
        lax.all_gather(w_o.astype(jnp.bfloat16), ("outer", "dp"), axis=0, tiled=True),
        lax.all_gather(w_in.astype(jnp.bfloat16), ("outer", "dp"), axis=0, tiled=True),
        lax.all_gather(w_out.astype(jnp.bfloat16), ("outer", "dp"), axis=0, tiled=True),
        lax.all_gather(vectors.astype(jnp.bfloat16), ("outer", "dp"), axis=1, tiled=True),
    )
    table_full, position_full, qkv_full, proj_full, inner_full, outer_full, vector_full = gathered
    matrices = (qkv_full, proj_full, inner_full, outer_full)
    vector_rows = vector_full.astype(jnp.float32)
    pair_rows = query_ids.shape[0]
    length = query_ids.shape[1]
    model_width = table.shape[1]
    token_ids = jnp.concatenate([query_ids, passage_ids])
    token_mask = jnp.concatenate([query_mask, passage_mask])
    embedded = jnp.take(table_full, token_ids, axis=0).astype(jnp.float32)
    embedded = embedded + position_full.astype(jnp.float32)[None]
    hidden_two, _ = forward(matrices, vector_rows, embedded, token_mask)
    pooled = pool(hidden_two, token_mask)
    queries = pooled[:pair_rows]
    passages = pooled[pair_rows:]
    index_base = lax.axis_index(("outer", "dp")) * pair_rows
    own_rows = index_base + jnp.arange(pair_rows, dtype=jnp.int32)
    all_passages = lax.all_gather(passages, ("outer", "dp"), axis=0, tiled=True)

    def part_loss(query_rows, passage_rows):
        return info_loss(query_rows, passage_rows, own_rows, source, positive)

    loss_part, loss_back = jax.vjp(part_loss, queries, all_passages)
    grad_queries, grad_spread = loss_back(jnp.ones((), jnp.float32))
    grad_passages = lax.psum_scatter(grad_spread, ("outer", "dp"), scatter_dimension=0, tiled=True)
    loss_total = lax.psum(loss_part, ("outer", "dp"))
    summed = None
    input_grads = []
    for offset, grad_pooled in ((0, grad_queries), (pair_rows, grad_passages)):
        block_input = embedded[offset : offset + pair_rows]
        block_mask = token_mask[offset : offset + pair_rows]
        block_hidden, saved_state = forward(matrices, vector_rows, block_input, block_mask)
        _, pool_back = jax.vjp(lambda hidden: pool(hidden, block_mask), block_hidden)
        grad_hidden = pool_back(grad_pooled)[0]
        grad_input, grad_matrices, grad_vectors = backward(
            matrices, vector_rows, block_input, block_mask, saved_state, grad_hidden
        )
        input_grads.append(grad_input)
        grad_position = (
            jnp.zeros(position_full.shape, jnp.float32).at[:length].add(jnp.sum(grad_input, 0))
        )
        block_sums = (grad_position,) + grad_matrices + (grad_vectors,)
        summed = block_sums if summed is None else jax.tree.map(jnp.add, summed, block_sums)
    summed = (
        lax.psum_scatter(summed[0], ("outer", "dp"), scatter_dimension=0, tiled=True),
        lax.psum_scatter(summed[1], ("outer", "dp"), scatter_dimension=0, tiled=True),
        lax.psum_scatter(summed[2], ("outer", "dp"), scatter_dimension=0, tiled=True),
        lax.psum_scatter(summed[3], ("outer", "dp"), scatter_dimension=0, tiled=True),
        lax.psum_scatter(summed[4], ("outer", "dp"), scatter_dimension=0, tiled=True),
        lax.psum_scatter(summed[5], ("outer", "dp"), scatter_dimension=1, tiled=True),
    )
    flat_ids = token_ids.reshape(-1)
    flat_grads = jnp.concatenate(input_grads).reshape(-1, model_width)
    count = table.shape[0] * lax.axis_size(("outer", "dp"))
    inside = (flat_ids >= 0) & (flat_ids < count)
    table_grad = lax.psum_scatter(
        jnp.zeros((count, model_width), jnp.float32)
        .at[jnp.where(inside, flat_ids, count)]
        .add(flat_grads, mode="drop"),
        ("outer", "dp"),
        scatter_dimension=0,
        tiled=True,
    )
    gradients = (table_grad,) + tuple(summed)
    squares = jnp.zeros((), jnp.float32)
    for gradient in gradients:
        squares = squares + jnp.sum(gradient * gradient)
    grad_norm = jnp.sqrt(lax.psum(squares, ("outer", "dp")))
    factor = jnp.minimum(1.0, CLIP_LIMIT / (grad_norm + 1e-06))
    masters = (table, positions, w_qkv, w_o, w_in, w_out, vectors)
    firsts = (first_table, first_positions, first_qkv, first_o, first_in, first_out, first_vectors)
    seconds = (
        second_table,
        second_positions,
        second_qkv,
        second_o,
        second_in,
        second_out,
        second_vectors,
    )
    rates = (LEARN_RATE,) * 6 + (VECTOR_RATE,)
    decays = (WEIGHT_DECAY,) * 6 + (0.0,)
    new_masters, new_firsts, new_seconds = ([], [], [])
    for master, first, second, gradient, rate, decay in zip(
        masters, firsts, seconds, gradients, rates, decays
    ):
        clipped = gradient * factor
        first = BETA_FIRST * first + (1.0 - BETA_FIRST) * clipped
        second = BETA_SECOND * second + (1.0 - BETA_SECOND) * clipped * clipped
        ratio = (
            first
            / (1.0 - BETA_FIRST**STEP)
            / (jnp.sqrt(second / (1.0 - BETA_SECOND**STEP)) + EPSILON)
        )
        new_masters.append(master - rate * (ratio + decay * master))
        new_firsts.append(first)
        new_seconds.append(second)
    return (
        new_masters[0],
        new_masters[1],
        new_masters[2],
        new_masters[3],
        new_masters[4],
        new_masters[5],
        new_masters[6],
        new_firsts[0],
        new_firsts[1],
        new_firsts[2],
        new_firsts[3],
        new_firsts[4],
        new_firsts[5],
        new_firsts[6],
        new_seconds[0],
        new_seconds[1],
        new_seconds[2],
        new_seconds[3],
        new_seconds[4],
        new_seconds[5],
        new_seconds[6],
        loss_total,
        grad_norm,
    )


def solution(mesh):
    placed = (
        P(("outer", "dp"), None),
        P(("outer", "dp"), None),
        P(("outer", "dp"), None),
        P(("outer", "dp"), None),
        P(),
        P(),
        P(("outer", "dp"), None),
        P(("outer", "dp"), None),
        P(("outer", "dp"), None),
        P(("outer", "dp"), None),
        P(("outer", "dp"), None),
        P(("outer", "dp"), None),
        P(None, ("outer", "dp")),
        P(("outer", "dp"), None),
        P(("outer", "dp"), None),
        P(("outer", "dp"), None),
        P(("outer", "dp"), None),
        P(("outer", "dp"), None),
        P(("outer", "dp"), None),
        P(None, ("outer", "dp")),
        P(("outer", "dp"), None),
        P(("outer", "dp"), None),
        P(("outer", "dp"), None),
        P(("outer", "dp"), None),
        P(("outer", "dp"), None),
        P(("outer", "dp"), None),
        P(None, ("outer", "dp")),
    )
    return jax.shard_map(
        per_device,
        mesh=mesh,
        in_specs=placed,
        out_specs=(
            P(("outer", "dp"), None),
            P(("outer", "dp"), None),
            P(("outer", "dp"), None),
            P(("outer", "dp"), None),
            P(("outer", "dp"), None),
            P(("outer", "dp"), None),
            P(None, ("outer", "dp")),
            P(("outer", "dp"), None),
            P(("outer", "dp"), None),
            P(("outer", "dp"), None),
            P(("outer", "dp"), None),
            P(("outer", "dp"), None),
            P(("outer", "dp"), None),
            P(None, ("outer", "dp")),
            P(("outer", "dp"), None),
            P(("outer", "dp"), None),
            P(("outer", "dp"), None),
            P(("outer", "dp"), None),
            P(("outer", "dp"), None),
            P(("outer", "dp"), None),
            P(None, ("outer", "dp")),
            P(),
            P(),
        ),
        check_vma=False,
    )
```

profile of v0, /device:TPU:0, one launch (start us, length us, event | category | flops | bytes accessed | tf_op | source)
XLA Modules:
  0.0 2411.9 jit_solution(4235995761667491077)
XLA Ops:
  19.3 72.8 %all-gather = bf16[32,24,14]{1,2,0:T(8,128)(2,1)S(1)} all-gather(bf16[1,24,14]{1,2,0:T(8,128)(2,1)S(1)} %convert_bitcast_fusion), channel_id=1, replica_groups=mesh['outer'=4,'dp'=8] {'outer','dp'}, dimensions={0}, use_global_device_ids=true | all-gather | bytes 22176 | tf_op jit(solution)/shard_map/all_gather | solution.py:220
  94.0 77.3 %all_gather.25 = bf16[512,768]{1,0:T(8,128)(2,1)S(1)} all-gather(bf16[16,768]{1,0:T(8,128)(2,1)S(1)} %convert_element_type.279), channel_id=1, replica_groups=mesh['outer'=4,'dp'=8] {'outer','dp'}, dimensions={0}, use_global_device_ids=true | all-gather | bytes 811008 | tf_op jit(solution)/shard_map/all_gather | solution.py:215
  174.5 108.7 %all-gather.8.cloned.1.call-done = bf16[30720,768]{1,0:T(8,128)(2,1)} async-done(((bf16[960,768]{1,0:T(8,128)(2,1)}), bf16[30720,768]{1,0:T(8,128)(2,1)}) %all-gather.8.cloned.1.call-update) | async-done | bytes 47185936 | tf_op jit(solution)/shard_map/all_gather | solution.py:214
  283.2 19.0 gather_fusion
  306.8 39.0 %all-gather.10.cloned.1.call-done = bf16[768,2304]{1,0:T(8,128)(2,1)} async-done(((bf16[24,2304]{1,0:T(8,128)(2,1)}), bf16[768,2304]{1,0:T(8,128)(2,1)}) %all-gather.10.cloned.1.call-update) | async-done | bytes 3538960 | tf_op jit(solution)/shard_map/all_gather | solution.py:216
  385.1 6.6 copy.113
  391.7 8.8 reshape.1553
  400.5 6.6 fusion.254
  415.2 24.9 %fusion.263 = (f32[2,12,512]{2,1,0:T(8,128)S(1)}, f32[2,12,512,512]{2,3,1,0:T(8,128)}) fusion(pred[2,512]{1,0:T(4,128)(4,1)S(1)} %broadcast_compare_fusion, bf16[2,512,1,12,64]{1,0,4,3,2:T(2,128)(2,1)} %get-tuple-element.302, bf16[2,512,1,12,64]{1,0,4,3,2:T(2,128)(2,1)} %get-tuple-element.303), kind=kOutput, calls=%fused_computation.555 | convolution fusion | flops 830472704 | bytes 28361728 | tf_op jit(solution)/shard_map/sub | solution.py:63
  440.1 10.9 fusion.78
  460.6 8.2 fusion.85
  468.8 36.6 %fusion.60.clone.4 = bf16[1024,3072]{1,0:T(8,128)(2,1)} fusion(f32[3072]{0:T(1024)S(1)} %add.770, bf16[768,3072]{1,0:T(8,128)(2,1)} %all-gather.14.cloned.1.call-done, f32[1024,768]{1,0:T(8,128)S(1)} %copy-done.14, f32[768]{0:T(1024)S(1)} %get-tuple-element.204, f32[768]{0:T(1024)S(1)} %get-tuple-element.205, ...), kind=kOutput, calls=%fused_computation.10.clone.clone.clone.clone.clone.clone.1 | convolution fusion | flops 5043388416 | bytes 14182400 | tf_op jit(solution)/shard_map/dot_general | solution.py:38
  505.3 28.9 %all-gather.16.cloned.1.call-done = bf16[3072,768]{1,0:T(8,128)(2,1)} async-done(((bf16[96,768]{1,0:T(8,128)(2,1)}), bf16[3072,768]{1,0:T(8,128)(2,1)}) %all-gather.16.cloned.1.call-update) | async-done | bytes 4718608 | tf_op jit(solution)/shard_map/all_gather | solution.py:219
  534.3 8.8 fusion.265
  547.4 66.7 %all-gather.1 = f32[32,1,768]{2,1,0:T(1,128)S(1)} all-gather(f32[1,1,768]{2,1,0:T(1,128)S(1)} %get-tuple-element.322), channel_id=1, replica_groups=mesh['outer'=4,'dp'=8] {'outer','dp'}, dimensions={0}, use_global_device_ids=true | all-gather | bytes 101376 | tf_op jit(solution)/shard_map/all_gather | solution.py:238
  623.1 34.6 %multiply_convert_fusion.2 = (bf16[512,3072]{1,0:T(8,128)(2,1)S(1)}, f32[512,3072]{1,0:T(8,128)}, bf16[512,3072]{1,0:T(8,128)(2,1)S(1)}, f32[512,3072]{1,0:T(8,128)}, f32[512,3072]{1,0:T(8,128)}) fusion(f32[3072]{0:T(1024)S(1)} %add.770, f32[512,3072]{1,0:T(8,128)S(1)} %fusion.230, bf16[768,3072]{1,0:T(8,128)(2,1)S(1)} %bitcast.556, ...), kind=kOutput, calls=%fused_computation.56 | convolution fusion | flops 2625503232 | bytes 37771264 | tf_op jit(solution)/shard_map/dot_general | solution.py:38
  709.8 112.6 %all-reduce.11.cloned.1.call-done = f32[32,768]{1,0:T(8,128)} async-done(((f32[32,768]{1,0:T(8,128)}), f32[32,768]{1,0:T(8,128)}) %all-reduce.11.cloned.1.call-update) | async-done | bytes 98320
  836.9 17.9 convert_reduce_fusion
  872.2 6.8 fusion.82
  879.0 8.9 multiply_reduce_fusion
  887.9 6.8 multiply_convert_fusion
  902.5 6.8 fusion.79
  909.3 8.9 multiply_reduce_fusion.1
  918.2 7.0 multiply_convert_fusion.1
  982.1 29.5 %broadcast_in_dim.283 = f32[30720,768]{1,0:T(8,128)} broadcast(f32[]{:T(128)} %constant.455.clone.1), dimensions={} | broadcast | bytes 94371840 | tf_op jit(solution)/shard_map/broadcast_in_dim | solution.py:277
  1011.5 130.6 %scatter_fusion = f32[30720,768]{1,0:T(8,128)} fusion(f32[30720,768]{1,0:T(8,128)} %broadcast_in_dim.283, s32[1024]{0:T(1024)S(1)} %bitcast.538, f32[1024,768]{1,0:T(8,128)S(1)} %bitcast.491), kind=kCustom, calls=%fused_computation.1 | custom fusion | flops 786432 | bytes 9441280 | tf_op jit(solution)/shard_map/scatter-add | solution.py:279
  1153.7 41.4 %all-reduce.7 = f32[14,768]{1,0:T(8,128)S(1)} all-reduce(f32[14,768]{1,0:T(8,128)S(1)} %add.842), channel_id=9, replica_groups=mesh['outer'=4,'dp'=8] {'outer','dp'}, use_global_device_ids=true, to_apply=%region_118.119.clone | all-reduce | flops 10752 | bytes 86016
  1198.8 70.3 %reduce-scatter.12.cloned.1.call-done = f32[24,2304]{1,0:T(8,128)} async-done(((f32[768,2304]{1,0:T(8,128)}), f32[24,2304]{1,0:T(8,128)}) %reduce-scatter.12.cloned.1.call-update) | async-done | bytes 221200 | tf_op jit(solution)/shard_map/reduce_scatter | solution.py:266
  1270.7 139.1 %reduce-scatter.18.cloned.1.call-done = f32[96,768]{1,0:T(8,128)} async-done(((f32[3072,768]{1,0:T(8,128)}), f32[96,768]{1,0:T(8,128)}) %reduce-scatter.18.cloned.1.call-update) | async-done | bytes 294928 | tf_op jit(solution)/shard_map/reduce_scatter | solution.py:269
  1411.4 139.9 %reduce-scatter.16.cloned.1.call-done = f32[24,3072]{1,0:T(8,128)} async-done(((f32[768,3072]{1,0:T(8,128)}), f32[24,3072]{1,0:T(8,128)}) %reduce-scatter.16.cloned.1.call-update) | async-done | bytes 294928 | tf_op jit(solution)/shard_map/reduce_scatter | solution.py:268
  1552.9 784.6 %reduce-scatter.8.cloned.1.call-done = f32[960,768]{1,0:T(8,128)} async-done(((f32[30720,768]{1,0:T(8,128)}), f32[960,768]{1,0:T(8,128)}) %reduce-scatter.8.cloned.1.call-update) | async-done | bytes 2949136 | tf_op jit(solution)/shard_map/reduce_scatter | solution.py:276
  2345.4 40.2 %all-reduce.8 = (f32[]{:T(128)}, f32[]{:T(128)}) all-reduce(f32[]{:T(128)S(6)} %add.843, f32[]{:T(128)} %bitcast.147), channel_id=1, replica_groups=mesh['outer'=4,'dp'=8] {'outer','dp'}, use_global_device_ids=true, to_apply=%region_120.121 | all-reduce | flops 2 | bytes 16 | tf_op jit(solution)/shard_map/psum | solution.py:288
  (562 shorter events, 250.5 us)
Async XLA Ops:
  7.3 275.9 %all-gather.8.cloned.1.call-start = ((), (), s32[]{:S(2)}) async-start(), calls=%async_computation.6 | async-start | bytes 48660480 | tf_op jit(solution)/shard_map/all_gather | solution.py:214
  10.6 83.4 %copy-start.57 = (f32[16,768]{1,0:T(8,128)S(1)}, f32[16,768]{1,0:T(8,128)}, u32[]{:S(2)}) copy-start(f32[16,768]{1,0:T(8,128)} %param.50) | copy-start | bytes 147460
  10.6 162.0 %copy-start.118 = (s32[32]{0:T(128)S(1)}, s32[32]{0:T(128)}, u32[]{:S(2)}) copy-start(s32[32]{0:T(128)} %param.47) | copy-start | bytes 388
  10.6 335.2 %all-gather.10.cloned.1.call-start = ((), (), s32[]{:S(2)}) async-start(), calls=%async_computation.7 | async-start | bytes 3649536 | tf_op jit(solution)/shard_map/all_gather | solution.py:216
  11.4 442.9 %all-gather.12.cloned.1.call-start = ((), (), s32[]{:S(2)}) async-start(), calls=%async_computation.8 | async-start | bytes 1216512 | tf_op jit(solution)/shard_map/all_gather | solution.py:217
  12.1 456.7 %all-gather.14.cloned.1.call-start = ((), (), s32[]{:S(2)}) async-start(), calls=%async_computation.9 | async-start | bytes 4866048 | tf_op jit(solution)/shard_map/all_gather | solution.py:218
  12.9 521.4 %all-gather.16.cloned.1.call-start = ((), (), s32[]{:S(2)}) async-start(), calls=%async_computation.10 | async-start | bytes 4866048 | tf_op jit(solution)/shard_map/all_gather | solution.py:219
  13.6 808.8 %all-reduce.11.cloned.1.call-start = ((), (), s32[]{:S(2)}) async-start(), calls=%async_computation.17 | async-start | bytes 196608
  93.2 361.1 %copy-start.59 = (f32[768]{0:T(1024)}, f32[768]{0:T(1024)S(1)}, u32[]{:S(2)}) copy-start(f32[768]{0:T(1024)S(1)} %get-tuple-element.210) | copy-start | bytes 9220
  93.2 361.1 %copy-start.63 = (f32[768]{0:T(1024)}, f32[768]{0:T(1024)S(1)}, u32[]{:S(2)}) copy-start(f32[768]{0:T(1024)S(1)} %get-tuple-element.209) | copy-start | bytes 9220
  93.2 361.1 %copy-start.85 = (f32[768]{0:T(1024)}, f32[768]{0:T(1024)S(1)}, u32[]{:S(2)}) copy-start(f32[768]{0:T(1024)S(1)} %get-tuple-element.206) | copy-start | bytes 9220
  543.2 72.6 %copy-start.3 = (f32[2,512,768]{2,1,0:T(8,128)S(1)}, f32[2,512,768]{2,1,0:T(8,128)}, u32[]{:S(2)}) copy-start(f32[2,512,768]{2,1,0:T(8,128)} %copy-done.2) | copy-start | bytes 9437188
  543.2 72.5 %copy-start.46 = (bf16[768,768]{1,0:T(8,128)(2,1)S(1)}, bf16[768,768]{1,0:T(8,128)(2,1)}, u32[]{:S(2)}) copy-start(bf16[768,768]{1,0:T(8,128)(2,1)} %all-gather.12.cloned.1.call-done) | copy-start | bytes 3538948
  543.2 72.5 %copy-start.53 = (bf16[12,64,512]{2,1,0:T(8,128)(2,1)S(1)}, bf16[12,64,512]{2,1,0:T(8,128)(2,1)}, u32[]{:S(2)}) copy-start(bf16[12,64,512]{2,1,0:T(8,128)(2,1)} %fusion.86) | copy-start | bytes 2359300
  543.2 72.5 %copy-start.60 = (f32[768]{0:T(1024)S(1)}, f32[768]{0:T(1024)}, u32[]{:S(2)}) copy-start(f32[768]{0:T(1024)} %copy-done.59) | copy-start | bytes 9220
  543.2 72.5 %copy-start.64 = (f32[768]{0:T(1024)S(1)}, f32[768]{0:T(1024)}, u32[]{:S(2)}) copy-start(f32[768]{0:T(1024)} %copy-done.63) | copy-start | bytes 9220
  543.2 72.5 %copy-start.73 = (f32[512]{0:T(512)S(1)}, f32[512]{0:T(512)}, u32[]{:S(2)}) copy-start(f32[512]{0:T(512)} %copy-done.72) | copy-start | bytes 6148
  543.2 72.5 %copy-start.86 = (f32[768]{0:T(1024)S(1)}, f32[768]{0:T(1024)}, u32[]{:S(2)}) copy-start(f32[768]{0:T(1024)} %copy-done.85) | copy-start | bytes 9220
  670.8 158.7 %copy-start.107 = (f32[32]{0:T(128)}, f32[32]{0:T(128)S(1)}, u32[]{:S(2)}) copy-start(f32[32]{0:T(128)S(1)} %get-tuple-element.365) | copy-start | bytes 388
  671.7 157.8 %copy-start.109 = (f32[32]{0:T(128)}, f32[32]{0:T(128)S(1)}, u32[]{:S(2)}) copy-start(f32[32]{0:T(128)S(1)} %get-tuple-element.367) | copy-start | bytes 388
  682.9 146.6 %copy-start.111 = (f32[32]{0:T(128)}, f32[32]{0:T(128)S(1)}, u32[]{:S(2)}) copy-start(f32[32]{0:T(128)S(1)} %get-tuple-element.363) | copy-start | bytes 388
  704.5 491.4 %reduce-scatter.10.cloned.1.call-start = ((), (), s32[]{:S(2)}) async-start(), calls=%async_computation.12 | async-start | bytes 1622016 | tf_op jit(solution)/shard_map/reduce_scatter | solution.py:265
  942.4 254.8 %reduce-scatter.14.cloned.1.call-start = ((), (), s32[]{:S(2)}) async-start(), calls=%async_computation.14 | async-start | bytes 2433024 | tf_op jit(solution)/shard_map/reduce_scatter | solution.py:267
  947.0 322.0 %reduce-scatter.12.cloned.1.call-start = ((), (), s32[]{:S(2)}) async-start(), calls=%async_computation.13 | async-start | bytes 7299072 | tf_op jit(solution)/shard_map/reduce_scatter | solution.py:266
  956.7 453.1 %reduce-scatter.18.cloned.1.call-start = ((), (), s32[]{:S(2)}) async-start(), calls=%async_computation.16 | async-start | bytes 9732096 | tf_op jit(solution)/shard_map/reduce_scatter | solution.py:269
  967.1 584.1 %reduce-scatter.16.cloned.1.call-start = ((), (), s32[]{:S(2)}) async-start(), calls=%async_computation.15 | async-start | bytes 9732096 | tf_op jit(solution)/shard_map/reduce_scatter | solution.py:268
  979.3 1358.2 %reduce-scatter.8.cloned.1.call-start = ((), (), s32[]{:S(2)}) async-start(), calls=%async_computation.11 | async-start | bytes 97320960 | tf_op jit(solution)/shard_map/reduce_scatter | solution.py:276
  1142.4 1243.9 %copy-start.78 = (f32[14,24]{1,0:T(8,128)S(1)}, f32[14,24]{1,0:T(8,128)}, u32[]{:S(2)}) copy-start(f32[14,24]{1,0:T(8,128)} %param.55) | copy-start | bytes 4036
  1142.4 1243.9 %copy-start.106 = (f32[14,24]{1,0:T(8,128)S(1)}, f32[14,24]{1,0:T(8,128)}, u32[]{:S(2)}) copy-start(f32[14,24]{1,0:T(8,128)} %param.62) | copy-start | bytes 4036
  1195.2 357.7 %copy-start.62 = (f32[14,768]{1,0:T(8,128)}, f32[14,768]{1,0:T(8,128)S(1)}, u32[]{:S(2)}) copy-start(f32[14,768]{1,0:T(8,128)S(1)} %all-reduce.7) | copy-start | bytes 129028
  1198.8 1194.7 %copy-start.42 = (f32[96,768]{1,0:T(8,128)S(1)}, f32[96,768]{1,0:T(8,128)}, u32[]{:S(2)}) copy-start(f32[96,768]{1,0:T(8,128)} %param.54) | copy-start | bytes 884740
  1552.9 842.7 %copy-start.44 = (f32[24,3072]{1,0:T(8,128)S(1)}, f32[24,3072]{1,0:T(8,128)}, u32[]{:S(2)}) copy-start(f32[24,3072]{1,0:T(8,128)} %param.53) | copy-start | bytes 884740
  (122 other events, 1386.0 us)
Sparse Core Ops, SparseCore 0:
  11.6 271.5 all-gather.7
  286.7 59.0 all-gather.9
  349.3 52.9 all-gather.11
  405.7 62.5 all-gather.13
  471.6 62.6 all-gather.15
  704.6 117.7 all-reduce.10
  942.6 97.8 reduce-scatter.9
  1046.3 98.0 reduce-scatter.13
  1151.0 118.0 reduce-scatter.11
  1274.8 134.8 reduce-scatter.17
  1416.7 134.5 reduce-scatter.15
  1557.5 779.8 reduce-scatter.7
where the time goes:
time: 2430 us; the launch traced here: 2410 us
  waiting for transfers between devices  1420 us (58%)
  blocking collectives  298 us (12%)
  matrix products  286 us (12%)
  other arithmetic  242 us (10%)
  local copies, waits for them, and re-layouts  109 us (4%)
  between operations  51.8 us (2%)
    reduce_scatter x1, waiting for transfers between devices, per_device(): lax.psum_scatter(jnp.zeros((count, model_width), jnp.float32).at[jnp.wher...  785 us
    dot_general x28, matrix products, matmul(): return jnp.dot(left, right, preferred_element_type=jnp.float32)  186 us
    reduce_scatter x1, waiting for transfers between devices, per_device(): lax.psum_scatter(summed[3], ('outer', 'dp'), scatter_dimension=0, tiled=T...  140 us
    reduce_scatter x1, waiting for transfers between devices, per_device(): lax.psum_scatter(summed[4], ('outer', 'dp'), scatter_dimension=0, tiled=T...  139 us
    scatter-add x1, other arithmetic, per_device(): table_grad = lax.psum_scatter(jnp.zeros((count, model_width), jnp.float32...  131 us
    unnamed x13, waiting for transfers between devices  113 us
    all_gather x1, waiting for transfers between devices, per_device(): lax.all_gather(table.astype(jnp.bfloat16), ('outer', 'dp'), axis=0, tiled...  109 us
    all_gather x1, blocking collectives, per_device(): lax.all_gather(positions.astype(jnp.bfloat16), ('outer', 'dp'), axis=0, t...  77.3 us
  transfers between devices with their start and end apart: 12, of which 8 were waited for; matrix products, arithmetic and copies ran while one was open for 17% of the time, Pallas kernels for 0%

commit v1 on v0

v1 whole, which is shorter than its diff:
```python
import functools

import jax
import jax.numpy as jnp
import numpy as np
from jax import lax
from jax.experimental import pallas as pl
from jax.experimental.pallas import tpu as pltpu
from jax.sharding import Mesh, PartitionSpec as P

D = 768
HEADS = 12
HEAD_DIM = 64
WIDTHS = (64, 128, 256, 768)
STEP = 10
TEMPER = 0.01
CLIP_LIMIT = 0.05
LEARN_RATE = 0.1
VECTOR_RATE = 0.3
BETA_FIRST = 0.9
BETA_SECOND = 0.999
WEIGHT_DECAY = 0.01
EPSILON = 1e-08
NORM_EPSILON = 1e-12
F32 = jnp.float32
BF16 = jnp.bfloat16
AXES = ("x", "core", "z", "y")
LANES = 128
MIB = 1024 * 1024


def matmul(left, right):
    return jnp.dot(left, right, preferred_element_type=F32)


def contract(left, right, left_dim, right_dim, precision=None):
    return lax.dot_general(
        left, right, (((left_dim,), (right_dim,)), ((), ())),
        precision=precision, preferred_element_type=F32,
    )


CHEAP = pl.CostEstimate(flops=1, bytes_accessed=1, transcendentals=0)
BLOCK = 256


def round_up(value, multiple):
    return -(-value // multiple) * multiple


def normalize(values):
    centre = values - jnp.mean(values, -1, keepdims=True)
    scale = lax.rsqrt(jnp.mean(centre * centre, -1, keepdims=True) + NORM_EPSILON)
    return centre * scale, scale


def normalize_back(grad_out, gain_row, normal, scale):
    grad = grad_out * gain_row
    return scale * (
        grad
        - jnp.mean(grad, -1, keepdims=True)
        - normal * jnp.mean(grad * normal, -1, keepdims=True)
    )


def column_sum(values):
    return jnp.sum(values, 0, keepdims=True)


def row_blocks(width, offset=0):
    return pl.BlockSpec((BLOCK, width), lambda i: (i, offset))


def fixed(shape, *index):
    index = index or (0,) * len(shape)
    return pl.BlockSpec(shape, lambda i: index, pipeline_mode=pl.Buffered(1))


def weight_blocks(first, count):
    return [fixed((D, D), 0, first + part) for part in range(count)]


def weight_row_blocks(count):
    return [fixed((D, D), part, 0) for part in range(count)]


ROOMY = ("update", "finish", "pieces", "lookup", "assemble", "assemble_pair", "grad_packed", "layer_back", "layer", "split_packed", "enter", "vec",)


def call(kernel, name, grid, in_specs, out_specs, out_shape, scratch=(), vmem=36):
    vmem = 60 if name in ROOMY else vmem
    return pl.pallas_call(
        kernel,
        grid=grid,
        in_specs=in_specs,
        out_specs=out_specs,
        out_shape=out_shape,
        scratch_shapes=scratch,
        cost_estimate=CHEAP,
        compiler_params=pltpu.CompilerParams(vmem_limit_bytes=vmem * MIB),
        name=name,
    )


def shape(rows, width, dtype):
    return jax.ShapeDtypeStruct((rows, width), dtype)


def pair_kernel(w_in, w_out, out_ref):
    pieces, rows = out_ref.shape[0] // 2, out_ref.shape[1]
    for piece in range(pieces):
        out_ref[piece] = w_in[:, piece * D : (piece + 1) * D].astype(BF16)
        out_ref[pieces + piece] = w_out[piece * rows : (piece + 1) * rows].astype(BF16)


def pair_of(w_in, w_out):
    rows, pieces = w_in.shape[0], w_in.shape[1] // D
    return call(
        pair_kernel, "pair", (1,), [fixed(w_in.shape), fixed(w_out.shape)], fixed((2 * pieces, rows, D)),
        jax.ShapeDtypeStruct((2 * pieces, rows, D), BF16),
    )(w_in, w_out)


def pieces_kernel(w_qkv, w_o, positions, vectors, w_in, w_out, out_ref):
    rows = out_ref.shape[1]
    small = [positions[...], vectors[...]]
    rest = rows - sum(part.shape[0] for part in small)
    if rest:
        small.append(jnp.zeros((rest, D), F32))
    parts = [w_qkv[:, piece * D : (piece + 1) * D] for piece in range(3)]
    parts += [w_o[...], jnp.concatenate(small, 0)]
    parts += [w_in[:, first : first + D] for first in range(0, w_in.shape[1], D)]
    parts += [w_out[first : first + rows] for first in range(0, w_out.shape[0], rows)]
    for piece, part in enumerate(parts):
        out_ref[piece] = part.astype(BF16)


def pieces_of(*parts):
    rows = parts[0].shape[0]
    extent = (5 + parts[4].shape[1] // D + parts[5].shape[0] // rows, rows, D)
    return call(
        pieces_kernel, "pieces", (1,), [fixed(part.shape) for part in parts], fixed(extent),
        jax.ShapeDtypeStruct(extent, BF16),
    )(*parts)


def vec_kernel(skip, width, rows, small, vec_ref):
    index = lambda axis: lax.broadcasted_iota(jnp.int32, (D, D), axis)
    mark = lambda chosen: jnp.where(chosen, 1.0, 0.0).astype(BF16)
    spot, column = index(0), index(1)
    held = matmul(mark(column == spot // width * rows + skip), small[...])
    held = jnp.where(column % width == spot % width, held, 0.0).astype(BF16)
    lanes = lax.broadcasted_iota(jnp.int32, (D, LANES), 1)
    part = lax.broadcasted_iota(jnp.int32, (D, LANES), 0) // width
    vec_ref[...] = matmul(held, mark(part == lanes)).T[: vec_ref.shape[0]]


def vec_of(gathered, count, width, skip, rows):
    return call(
        functools.partial(vec_kernel, skip, width, rows), "vec", (1,),
        [pl.BlockSpec((D, D), lambda i: (0, 4))], fixed((round_up(count, 8), D)),
        shape(round_up(count, 8), D, F32),
    )(gathered)


def plan_kernel(owned, room, query_ids, passage_ids, slot_column, slot_row, rank_row, fresh_row, wanted):
    tokens = slot_row.shape[1]
    row = [ref[index : index + 1, :] for ref in (query_ids, passage_ids) for index in range(ref.shape[0])]
    row = jnp.concatenate(row, 1)
    column = jnp.broadcast_to(row.astype(F32), (8, tokens)).T[:, :1].astype(jnp.int32)
    down = lax.broadcasted_iota(jnp.int32, (tokens, tokens), 0)
    across = lax.broadcasted_iota(jnp.int32, (tokens, tokens), 1)
    count = lambda chosen, axis: jnp.sum(jnp.where(chosen, 1, 0), axis, keepdims=True)
    equal = column == row
    new_column = count(equal & (across < down), 1) == 0
    new_row = count(equal & (down < across), 0) == 0
    holder_column, holder_row = column // owned, row // owned
    together = holder_column == holder_row
    rank_of_column = count(together & (row < column) & new_row, 1)
    rank_of_row = count(together & (column < row) & new_column, 0)
    slot = lambda holder, rank: jnp.where(rank < room - 1, holder * room + rank, -1)
    slot_column[...] = slot(holder_column, rank_of_column)
    slot_row[...] = slot(holder_row, rank_of_row)
    rank_row[...] = rank_of_row
    fresh_row[...] = jnp.where(new_row, 1, 0)
    devices = wanted.shape[0]
    mine = (lax.broadcasted_iota(jnp.int32, (devices, tokens), 0) == holder_row) & new_row
    lanes = lax.broadcasted_iota(jnp.int32, (tokens, LANES), 1)
    spots = jnp.where((rank_of_column == lanes) & (lanes < room - 1), 1.0, 0.0).astype(BF16)
    ask = row - holder_row * owned + 1
    high = ask // 64
    pick = lambda values: matmul(jnp.where(mine, values, 0).astype(F32).astype(BF16), spots)
    asks = pick(high) * 64.0 + pick(ask - high * 64)
    deepest = jnp.max(rank_of_row, 1, keepdims=True)
    lanes = lax.broadcasted_iota(jnp.int32, (devices, LANES), 1)
    wanted[...] = jnp.where(lanes == LANES - 1, deepest, asks.astype(jnp.int32))


def plan_of(query_ids, passage_ids, owned, room, devices):
    tokens = query_ids.size + passage_ids.size
    ints = lambda *extent: jax.ShapeDtypeStruct(extent, jnp.int32)
    row = fixed((1, tokens))
    return call(
        functools.partial(plan_kernel, owned, room), "plan", (1,),
        [fixed(query_ids.shape), fixed(passage_ids.shape)],
        [fixed((tokens, 1)), row, row, row, fixed((devices, LANES))],
        [ints(tokens, 1), ints(1, tokens), ints(1, tokens), ints(1, tokens), ints(devices, LANES)],
    )(query_ids, passage_ids)


def lookup_kernel(room, asked, table, chosen_ref, found_ref):
    asks = asked[...].astype(F32).T
    devices, owned = asked.shape[0], table.shape[0]
    rows = lax.broadcasted_iota(jnp.int32, (room, owned), 1).astype(F32) + 1.0
    for device in range(0, devices, 2):
        both = [jnp.where(asks[:room, side : side + 1] == rows, 1.0, 0.0) for side in (device, device + 1)]
        chosen_ref[device * room : (device + 2) * room] = jnp.concatenate(both, 0).astype(BF16)
    found_ref[...] = matmul(chosen_ref[...], table[...].astype(BF16)).astype(BF16)


def lookup(asked, table, room):
    slots = asked.shape[0] * room
    owned = table.shape[0]
    return call(
        functools.partial(lookup_kernel, room), "lookup", (1,),
        [fixed(asked.shape), fixed(table.shape)],
        [fixed((slots, owned)), fixed((slots, D))],
        [shape(slots, owned, BF16), shape(slots, D, BF16)],
    )(asked, table)


def take_kernel(chosen, given, grad_ref):
    grad_ref[...] = contract(chosen[...], given[...], 0, 0)


def take_rows(chosen, given):
    owned = chosen.shape[1]
    return call(
        take_kernel, "take", (1,), [fixed(chosen.shape), fixed(given.shape)], fixed((owned, D)),
        shape(owned, D, F32),
    )(chosen, given)


def enter_kernel(place_rows, rows, slot_ref, found_ref, x_ref, place_ref, vec_ref, wq_ref, wk_ref, wv_ref, normal_ref, scale_ref, low_ref, packed_ref):
    places = place_ref[...].astype(F32)
    places = [places[first : first + place_rows] for first in range(0, places.shape[0], rows)]
    places = jnp.concatenate(places, 0) + x_ref[...]
    slots = lax.broadcasted_iota(jnp.int32, (BLOCK, found_ref.shape[0]), 1)
    chosen = jnp.where(slot_ref[...] == slots, 1.0, 0.0).astype(BF16)
    normal, scale = normalize(matmul(chosen, found_ref[...]) + places)
    low = (normal * vec_ref[8:9] + vec_ref[9:10]).astype(BF16)
    normal_ref[...], scale_ref[...], low_ref[...] = normal, scale, low
    for part, (weight, bias) in enumerate(((wq_ref, 0), (wk_ref, None), (wv_ref, 1))):
        out = matmul(low, weight[...])
        if bias is not None:
            out = out + vec_ref[bias : bias + 1]
        packed_ref[:, part * D : (part + 1) * D] = out.astype(BF16)


def enter(slot, found, looked_up, vec, gathered, length, place_rows, rows):
    tokens = looked_up.shape[0]
    cycle = length // BLOCK
    place_block = pl.BlockSpec((BLOCK // place_rows * rows, D), lambda i: (i % cycle, 4))
    return call(
        functools.partial(enter_kernel, place_rows, rows), "enter", (tokens // BLOCK,),
        [row_blocks(1), fixed(found.shape), row_blocks(D), place_block, fixed(vec.shape)]
        + weight_blocks(0, 3),
        [row_blocks(D), row_blocks(1), row_blocks(D), row_blocks(3 * D)],
        [shape(tokens, D, F32), shape(tokens, 1, F32), shape(tokens, D, BF16), shape(tokens, 3 * D, BF16)],
    )(slot, found, looked_up, gathered, vec, *[gathered] * 3)


def layer_kernel(cycle, pieces, *refs):
    normal_zero, context, share, vec, w_o = refs[:5]
    w_in, w_out = refs[5 : 5 + pieces], refs[5 + pieces : 5 + 2 * pieces]
    normal_one_ref, scale_one_ref, low_one_ref, active_ref, slope_ref = refs[5 + 2 * pieces : 10 + 2 * pieces]
    normal_two_ref, scale_two_ref, pooled_ref = refs[10 + 2 * pieces :]
    hidden = normal_zero[...] * vec[8:9] + vec[9:10]
    normal_one, scale_one = normalize(hidden + matmul(context[...], w_o[...]) + vec[2:3])
    hidden = normal_one * vec[10:11] + vec[11:12]
    low = hidden.astype(BF16)
    normal_one_ref[...], scale_one_ref[...], low_one_ref[...] = normal_one, scale_one, low
    total = hidden + vec[7:8]
    for part in range(pieces):
        columns = slice(part * D, (part + 1) * D)
        inner = matmul(low, w_in[part][...]) + vec[3 + part : 4 + part]
        gate = 0.5 + 0.5 * lax.erf(inner * (0.5**0.5))
        active = (inner * gate).astype(BF16)
        active_ref[:, columns] = active
        slope_ref[:, columns] = gate + inner * jnp.exp(-0.5 * inner * inner) * (2.0 * np.pi) ** -0.5
        total = total + matmul(active, w_out[part][...])
    normal_two, scale_two = normalize(total)
    normal_two_ref[...], scale_two_ref[...] = normal_two, scale_two
    pooled = column_sum((normal_two * vec[12:13] + vec[13:14]) * share[...])

    @pl.when(pl.program_id(0) % cycle == 0)
    def _():
        pooled_ref[0] = jnp.zeros((1, D), F32)

    pooled_ref[0] += pooled


def layer(normal_zero, context, share, vec, gathered, w_in, w_out, length):
    tokens, units = normal_zero.shape[0], w_in.shape[1]
    cycle, pieces = length // BLOCK, units // D
    return call(
        functools.partial(layer_kernel, cycle, pieces), "layer", (tokens // BLOCK,),
        [row_blocks(D), row_blocks(D), row_blocks(1), fixed(vec.shape)]
        + weight_blocks(3, 1) + weight_blocks(0, pieces) + weight_row_blocks(pieces),
        [row_blocks(D), row_blocks(1), row_blocks(D), row_blocks(units), row_blocks(units)]
        + [row_blocks(D), row_blocks(1), pl.BlockSpec((1, 1, D), lambda i: (i // cycle, 0, 0))],
        [shape(tokens, D, F32), shape(tokens, 1, F32), shape(tokens, D, BF16)]
        + [shape(tokens, units, BF16), shape(tokens, units, F32)]
        + [shape(tokens, D, F32), shape(tokens, 1, F32)]
        + [jax.ShapeDtypeStruct((tokens // length, 1, D), F32)],
    )(normal_zero, context, share, vec, gathered, *[w_in] * pieces, *[w_out] * pieces)


def layer_back_kernel(pieces, *refs):
    grad_pooled, share, normal_two, scale_two, slope, normal_one, scale_one, vec, w_o = refs[:9]
    w_in, w_out = refs[9 : 9 + pieces], refs[9 + pieces : 9 + 2 * pieces]
    inner_ref, mixed_ref, attended_ref, context_ref, sums_ref = refs[9 + 2 * pieces :]
    grad_hidden = share[...] * grad_pooled[0]
    grad_two = normalize_back(grad_hidden, vec[12:13], normal_two[...], scale_two[...])
    branch = grad_two.astype(BF16)
    sums = []
    total = grad_two
    for part in range(pieces):
        columns = slice(part * D, (part + 1) * D)
        inner = (contract(branch, w_out[part][...], 1, 1) * slope[:, columns]).astype(BF16)
        inner_ref[:, columns] = inner
        sums.append(column_sum(inner.astype(F32)))
        total = total + contract(inner, w_in[part][...], 1, 1)
    mixed = normalize_back(total, vec[10:11], normal_one[...], scale_one[...])
    mixed_ref[...] = mixed
    attended = mixed.astype(BF16)
    attended_ref[...] = attended
    context_ref[...] = contract(attended, w_o[...], 1, 1).astype(BF16)
    sums += [
        column_sum(branch.astype(F32)),
        column_sum(total * normal_one[...]), column_sum(total),
        column_sum(grad_hidden * normal_two[...]), column_sum(grad_hidden),
        column_sum(attended.astype(F32)),
    ]
    sums += [jnp.zeros((1, D), F32)] * (sums_ref.shape[0] - len(sums))

    @pl.when(pl.program_id(0) == 0)
    def _():
        sums_ref[...] = jnp.zeros_like(sums_ref)

    sums_ref[...] += jnp.concatenate(sums, 0)


def layer_back(grad_pooled, share, normal_two, scale_two, slope, normal_one, scale_one, vec, gathered, w_in, w_out, length):
    tokens, units = slope.shape
    cycle, pieces = length // BLOCK, units // D
    return call(
        functools.partial(layer_back_kernel, pieces), "layer_back", (tokens // BLOCK,),
        [pl.BlockSpec((1, 1, D), lambda i: (i // cycle, 0, 0)), row_blocks(1), row_blocks(D), row_blocks(1)]
        + [row_blocks(units), row_blocks(D), row_blocks(1), fixed(vec.shape)]
        + weight_blocks(3, 1) + weight_blocks(0, pieces) + weight_row_blocks(pieces),
        [row_blocks(units), row_blocks(D), row_blocks(D), row_blocks(D), fixed((16, D))],
        [shape(tokens, units, BF16), shape(tokens, D, F32), shape(tokens, D, BF16)]
        + [shape(tokens, D, BF16), shape(16, D, F32)],
    )(grad_pooled, share, normal_two, scale_two, slope, normal_one, scale_one, vec, gathered, *[w_in] * pieces, *[w_out] * pieces)


def leave_kernel(place_rows, packed, mixed, normal, scale, vec, wq, wk, wv, low_ref, place_ref, sums_ref):
    total = mixed[...]
    for part, weight in enumerate((wq, wk, wv)):
        total = total + contract(packed[:, part * D : (part + 1) * D], weight[...], 1, 1)
    grad = normalize_back(total, vec[8:9], normal[...], scale[...])
    low_ref[...] = grad.astype(BF16)

    @pl.when(pl.program_id(1) == 0)
    def _():
        place_ref[...] = jnp.zeros_like(place_ref)

    places = place_rows
    for device in range(place_ref.shape[0]):
        place_ref[device, :places] += grad[device * places : (device + 1) * places]

    @pl.when((pl.program_id(0) == 0) & (pl.program_id(1) == 0))
    def _():
        sums_ref[...] = jnp.zeros_like(sums_ref)

    sums = [
        column_sum(total * normal[...]), column_sum(total),
        column_sum(packed[:, :D].astype(F32)), column_sum(packed[:, 2 * D :].astype(F32)),
        jnp.zeros((4, D), F32),
    ]
    sums_ref[...] += jnp.concatenate(sums, 0)


def leave(grad_packed, grad_mixed, normal, scale, vec, gathered, length, place_rows, rows):
    tokens = grad_mixed.shape[0]
    cycle = length // BLOCK
    blocks = lambda width: pl.BlockSpec((BLOCK, width), lambda j, s: (s * cycle + j, 0))
    place_block = pl.BlockSpec((BLOCK // place_rows, rows, D), lambda j, s: (j, 0, 0))
    still = lambda size, *index: pl.BlockSpec(size, lambda j, s: index, pipeline_mode=pl.Buffered(1))
    return call(
        functools.partial(leave_kernel, place_rows), "leave", (cycle, tokens // length),
        [blocks(3 * D), blocks(D), blocks(D), blocks(1), still(vec.shape, 0, 0)]
        + [still((D, D), 0, part) for part in range(3)],
        [blocks(D), place_block, still((8, D), 0, 0)],
        [shape(tokens, D, BF16), jax.ShapeDtypeStruct((length // place_rows, rows, D), F32), shape(8, D, F32)],
    )(grad_packed, grad_mixed, normal, scale, vec, *[gathered] * 3)


def weight_grad_kernel(counts, with_extra, core, *refs):
    pairs, (extra, kept_ref, sent_ref, total_ref) = refs[: 2 * len(counts)], refs[2 * len(counts) :]
    _, width, _, depth, rows, _ = kept_ref.shape
    groups = kept_ref.shape[0]
    step = pl.program_id(0)
    first = 0
    for index, count in enumerate(counts):
        left, right = pairs[2 * index : 2 * index + 2]

        @pl.when((step >= first) & (step < first + count))
        def _():
            total_ref[...] = contract(left[...], right[...], 0, 0)

        first += count

    def store(read):
        for own in range(2):

            @pl.when(core[0] == own)
            def _():
                for x in range(groups):
                    for z in range(depth):
                        for y in range(width):
                            kept_ref[x, y, 0, z] = read(x, own, z, y)
                            sent_ref[x, y, 0, z] = read(x, 1 - own, z, y).astype(BF16)

    @pl.when(step < first)
    def _():
        place = lambda x, side, z, y: (((2 * x + side) * depth + z) * width + y) * rows
        store(lambda *at: total_ref[place(*at) : place(*at) + rows, :])

    if with_extra:

        @pl.when(step == first)
        def _():
            store(lambda *at: extra[at])


def weight_grad(name, pairs, core, sizes, extra=None):
    tokens = pairs[0][0].shape[0]
    counts = [right.shape[1] // D for _, right in pairs]
    pieces = sum(counts) + (extra is not None)
    rows = D // (2 * sizes[0] * sizes[1] * sizes[2])
    extent = (sizes[0], sizes[2], pieces, sizes[1], rows, D)
    specs, first = [pl.BlockSpec(memory_space=pltpu.SMEM)], 0
    for count in counts:
        specs.append(pl.BlockSpec((tokens, D), lambda k: (0, 0)))
        specs.append(
            pl.BlockSpec(
                (tokens, D),
                functools.partial(lambda first, last, k: (0, jnp.clip(k - first, 0, last)), first, count - 1),
            )
        )
        first += count
    with_extra = extra is not None
    if not with_extra:
        extra = jnp.zeros((8, LANES), F32)
    specs.append(pl.BlockSpec(extra.shape, lambda k: (0,) * extra.ndim))
    out = pl.BlockSpec(extent[:2] + (1,) + extent[3:], lambda k: (0, 0, k, 0, 0, 0))
    return call(
        functools.partial(weight_grad_kernel, counts, with_extra), name, (pieces,), specs,
        [out, out],
        [jax.ShapeDtypeStruct(extent, F32), jax.ShapeDtypeStruct(extent, BF16)],
        scratch=[pltpu.VMEM((D, D), F32)],
    )(core, *[side for pair in pairs for side in pair], extra)


def outer_grad_kernel(core, left, grad_pooled, share, normal, scale, vec, kept_ref, sent_ref, branch):
    @pl.when((pl.program_id(0) == 0) & (pl.program_id(1) == 0))
    def _():
        sequences = grad_pooled.shape[0]
        length = share.shape[0] // sequences
        for index in range(sequences):
            part = slice(index * length, (index + 1) * length)
            grad_hidden = share[part] * grad_pooled[index]
            branch[part] = normalize_back(grad_hidden, vec[12:13], normal[part], scale[part]).astype(BF16)

    total = contract(left[...], branch[...], 0, 0)
    _, width, pieces, depth, rows, _ = kept_ref.shape

    def store(ref):
        for z in range(depth):
            for y in range(width):
                for piece in range(pieces):
                    first = ((z * width + y) * pieces + piece) * rows
                    ref[0, y, piece, z] = total[first : first + rows].astype(ref.dtype)

    @pl.when(pl.program_id(1) == 0)
    def _():
        store(kept_ref)

    @pl.when(pl.program_id(1) == 1)
    def _():
        store(sent_ref)


def outer_grad(left, grad_pooled, share, normal, scale, vec, core, sizes, rows):
    tokens, units = left.shape
    width = units // (2 * sizes[0])
    extent = (sizes[0], sizes[2], width // (sizes[1] * sizes[2] * rows), sizes[1], rows, D)
    out = pl.BlockSpec((1,) + extent[1:], lambda x, side, core: (x, 0, 0, 0, 0, 0))
    still = lambda values: pl.BlockSpec(values.shape, lambda x, side, core: (0,) * values.ndim)
    return pl.pallas_call(
        outer_grad_kernel,
        grid_spec=pltpu.PrefetchScalarGridSpec(
            num_scalar_prefetch=1,
            grid=(sizes[0], 2),
            in_specs=[
                pl.BlockSpec((tokens, width), lambda x, side, core: (0, 2 * x + (core[0] + side) % 2)),
                still(grad_pooled), still(share), still(normal), still(scale), still(vec),
            ],
            out_specs=[out, out],
            scratch_shapes=[pltpu.VMEM((tokens, D), BF16)],
        ),
        out_shape=[jax.ShapeDtypeStruct(extent, F32), jax.ShapeDtypeStruct(extent, BF16)],
        cost_estimate=CHEAP,
        compiler_params=pltpu.CompilerParams(vmem_limit_bytes=36 * MIB),
        name="grad_outer",
    )(core, left, grad_pooled, share, normal, scale, vec)


def split_kernel(count, partners, *refs):
    inputs, outputs = refs[:count], refs[count:]
    for index, out in enumerate(outputs):
        part = partners[index]
        total = inputs[0][part, 0].astype(F32)
        for more in inputs[1:]:
            total = total + more[part, 0].astype(F32)
        out[0] = total.astype(out.dtype)


def split(name, values, partners):
    parts, pieces = values[0].shape[:2]
    rest = values[0].shape[2:]
    zeros = (0,) * len(rest)
    return call(
        functools.partial(split_kernel, len(values)), name, (pieces,),
        [pl.BlockSpec(memory_space=pltpu.SMEM)]
        + [pl.BlockSpec((parts, 1) + rest, lambda k: (0, k) + zeros)] * len(values),
        [pl.BlockSpec((1,) + rest, lambda k: (k,) + zeros)] * parts,
        [jax.ShapeDtypeStruct((pieces,) + rest, F32 if part == 0 else BF16) for part in range(parts)],
    )(partners, *values)


def fold_kernel(count, partners, *refs):
    inputs, outputs = refs[:count], refs[count:]
    for index, out in enumerate(outputs):
        part = partners[index]
        total = inputs[0][0, part]
        for more in inputs[1:]:
            total = total + more[0, part].astype(F32)
        out[0] = total.astype(out.dtype)


def fold(name, values, partners):
    pieces, parts, rows, _ = values[0].shape
    return call(
        functools.partial(fold_kernel, len(values)), name, (pieces,),
        [pl.BlockSpec(memory_space=pltpu.SMEM)]
        + [pl.BlockSpec((1, parts, rows, D), lambda k: (k, 0, 0, 0))] * len(values),
        [pl.BlockSpec((1, rows, D), lambda k: (k, 0, 0))] * parts,
        [jax.ShapeDtypeStruct((pieces, rows, D), F32 if part == 0 else BF16) for part in range(parts)],
    )(partners, *values)


def assemble_kernel(sources, width, counts, core, in_plane, *refs):
    inputs, outputs = refs[: -len(counts)], refs[-len(counts) :]
    for index in range(2 * sources):
        side = core[0] if index < sources else 1 - core[0]
        plane = in_plane[index % sources]
        x, y = plane // width, plane % width
        for place, out_ref in enumerate(outputs):
            ref = inputs[index * len(outputs) + place]
            for step in range(ref.shape[0]):
                if len(out_ref.shape) == 6:
                    out_ref[x, side, step, y] = ref[step, 0]
                else:
                    out_ref[x, side, step, y, 0] = ref[step, 0]


def assemble(name, own, came, core, in_plane, sizes, wide, tall=0):
    depth, _, rows, _ = own[0].shape
    smem = pl.BlockSpec(memory_space=pltpu.SMEM)
    block = lambda first: pl.BlockSpec((depth, 1, rows, D), lambda k: (0, first + k, 0, 0))
    extent = (sizes[0], 2, depth, sizes[2])
    outs = [pl.BlockSpec(extent + (rows, D), lambda k: (0, 0, 0, 0, 0, k))]
    shapes = [jax.ShapeDtypeStruct(extent + (rows, wide * D), BF16)]
    if tall:
        outs.append(pl.BlockSpec(extent + (1, rows, D), lambda k: (0, 0, 0, 0, k, 0, 0)))
        shapes.append(jax.ShapeDtypeStruct(extent + (tall, rows, D), BF16))
    parts = (*own, *came)
    firsts = (0, wide)[: len(outs)]
    made = call(
        functools.partial(assemble_kernel, len(own), sizes[2], (wide, tall)[: len(outs)]), name, (wide,),
        [smem, smem] + [block(first) for _ in parts for first in firsts],
        outs, shapes,
    )(core, in_plane, *[part for part in parts for _ in firsts])
    return [made[0].reshape(D, -1)] + [part.reshape(-1, D) for part in made[1:]]


def give_kernel(room, slot, grad, vectors, out_ref):
    first = pl.program_id(0) * out_ref.shape[0]
    rows = first + lax.broadcasted_iota(jnp.int32, (out_ref.shape[0], slot.shape[1]), 0)
    total = matmul(jnp.where(rows == slot[...], 1.0, 0.0).astype(BF16), grad[...])
    devices = vectors.shape[0]
    rows = first + lax.broadcasted_iota(jnp.int32, (out_ref.shape[0], devices), 0)
    last = lax.broadcasted_iota(jnp.int32, (out_ref.shape[0], devices), 1) * room + room - 1
    total = total + matmul(jnp.where(rows == last, 1.0, 0.0).astype(BF16), vectors[...])
    out_ref[...] = total.astype(BF16)


def give_rows(slot, grad, vectors, room):
    devices = vectors.shape[0]
    block = 8 * room
    return call(
        functools.partial(give_kernel, room), "give", (devices // 8,),
        [fixed(slot.shape), fixed(grad.shape), fixed(vectors.shape)],
        pl.BlockSpec((block, D), lambda i: (i, 0)),
        shape(devices * room, D, BF16),
    )(slot, grad, vectors)


PARTS = 2


def head_marks():
    half = lax.broadcasted_iota(jnp.int32, (1, LANES), 1) // HEAD_DIM
    return [jnp.where(half == head, 1.0, 0.0).astype(BF16) for head in range(2)]


def attend_kernel(mask_ref, q_ref, k_ref, v_ref, ctx_ref, lse_ref):
    keep = mask_ref[0] > 0
    lane = lax.broadcasted_iota(jnp.int32, (1, LANES), 1)
    scale = jnp.asarray(HEAD_DIM ** (-0.5), BF16)
    log_total = jnp.zeros(lse_ref.shape[1:], F32)
    for pair in range(q_ref.shape[1] // LANES):
        columns = slice(pair * LANES, (pair + 1) * LANES)
        queries, keys, values = q_ref[:, columns], k_ref[:, columns], v_ref[:, columns]
        context = jnp.zeros(queries.shape, F32)
        for head, own in enumerate(head_marks()):
            scores = contract(queries, keys * (own * scale), 1, 1)
            scores = jnp.where(keep, scores, -1000000000.0)
            peak = jnp.max(scores, 1, keepdims=True)
            exponent = jnp.exp(scores - peak)
            total = jnp.sum(exponent, 1, keepdims=True)
            weights = (exponent * (1.0 / total)).astype(BF16)
            context = context + matmul(weights, values * own)
            log_total = jnp.where(lane == 2 * pair + head, peak + jnp.log(total), log_total)
        ctx_ref[:, columns] = context.astype(BF16)
    lse_ref[0] = log_total


def attend_back_kernel(mask_ref, q_ref, k_ref, v_ref, dctx_ref, lse_ref, grad_ref):
    keep = mask_ref[0] > 0
    scale = HEAD_DIM ** (-0.5)
    width = q_ref.shape[1]
    for pair in range(width // LANES):
        columns = slice(pair * LANES, (pair + 1) * LANES)
        queries, keys, values, dctx = (ref[:, columns] for ref in (q_ref, k_ref, v_ref, dctx_ref))
        grad_q, grad_k, grad_v = (jnp.zeros(queries.shape, F32) for _ in range(3))
        for head, own in enumerate(head_marks()):
            own_keys = keys * (own * jnp.asarray(scale, BF16))
            own_dctx = dctx * own
            scores = contract(queries, own_keys, 1, 1)
            scores = jnp.where(keep, scores, -1000000000.0)
            spot = 2 * pair + head
            weights = jnp.exp(scores - lse_ref[0, :, spot : spot + 1])
            grad_weights = contract(own_dctx, values, 1, 1)
            inner = jnp.sum(grad_weights * weights, 1, keepdims=True)
            grad_scores = (weights * (grad_weights - inner)).astype(BF16)
            grad_q = grad_q + matmul(grad_scores, own_keys)
            grad_k = grad_k + contract(grad_scores, queries * own, 0, 0)
            grad_v = grad_v + contract(weights.astype(BF16), own_dctx, 0, 0)
        for part, grad in enumerate((grad_q, grad_k * scale, grad_v)):
            start = pl.multiple_of(part * D + pl.program_id(1) * width + pair * LANES, LANES)
            grad_ref[:, pl.ds(start, LANES)] = grad.astype(BF16)


def attend_specs(length):
    width = D // PARTS
    block = lambda part: pl.BlockSpec((length, width), lambda s, h: (s, part * PARTS + h))
    mask = pl.BlockSpec((1, 1, length), lambda s, h: (s, 0, 0))
    sums = pl.BlockSpec((1, length, LANES), lambda s, h: (h, s, 0))
    return [mask, block(0), block(1), block(2)], block(0), sums


def attend(packed, mask, sequences, length):
    tokens = sequences * length
    inputs, plain, sums = attend_specs(length)
    return call(
        attend_kernel, "attend", (sequences, PARTS), inputs, [plain, sums],
        [shape(tokens, D, BF16), jax.ShapeDtypeStruct((PARTS, tokens, LANES), F32)],
    )(mask, packed, packed, packed)


def attend_back(packed, mask, grad_context, log_total, sequences, length):
    inputs, plain, sums = attend_specs(length)
    return call(
        attend_back_kernel, "attend_back", (sequences, PARTS), inputs + [plain, sums],
        pl.BlockSpec((length, 3 * D), lambda s, h: (s, 0)),
        shape(sequences * length, 3 * D, BF16),
    )(mask, packed, packed, packed, grad_context, log_total)


def unit(values):
    scale = lax.rsqrt(jnp.sum(values * values, -1, keepdims=True) + NORM_EPSILON)
    return values * scale, scale


def loss_kernel(me, q_ref, p_ref, source_ref, positive_ref, loss_ref, grad_ref, all_ref):
    queries, query_scale = unit(q_ref[...])
    passages, passage_scale = unit(p_ref[...])
    count = queries.shape[0]
    precise = lax.Precision.HIGHEST
    feature = lax.broadcasted_iota(jnp.int32, (1, D), 1)
    chosen = lax.broadcasted_iota(jnp.int32, (count, count), 1) == positive_ref[...]
    source = source_ref[...]
    own_source = jnp.sum(jnp.where(chosen, source, 0), 1, keepdims=True)
    keeping = source == own_source
    loss = jnp.zeros((1, 1), F32)
    grad_q = jnp.zeros_like(queries)
    grad_p = jnp.zeros_like(passages)
    for width in WIDTHS:
        inside = feature < width
        left, left_scale = unit(jnp.where(inside, queries, 0.0))
        right, right_scale = unit(jnp.where(inside, passages, 0.0))
        scores = contract(left, right, 1, 1, precise) / TEMPER
        scores = jnp.where(keeping, scores, -1000000000.0)
        peak = jnp.max(scores, 1, keepdims=True)
        exponent = jnp.exp(scores - peak)
        total = jnp.sum(exponent, 1, keepdims=True)
        target = jnp.sum(jnp.where(chosen, scores, 0.0), 1, keepdims=True)
        loss = loss + jnp.sum(peak + jnp.log(total) - target, 0, keepdims=True)
        slope = jnp.where(keeping, exponent / total - jnp.where(chosen, 1.0, 0.0), 0.0)
        slope = slope * (1.0 / (TEMPER * count))
        grad_left = contract(slope, right, 1, 0, precise)
        grad_right = contract(slope, left, 0, 0, precise)
        grad_q = grad_q + left_scale * (
            grad_left - left * jnp.sum(grad_left * left, -1, keepdims=True)
        )
        grad_p = grad_p + right_scale * (
            grad_right - right * jnp.sum(grad_right * right, -1, keepdims=True)
        )
    loss_ref[...] = loss / count
    own = grad_ref.shape[0] // 2
    for side, (grad, values, scale) in enumerate(
        ((grad_q, queries, query_scale), (grad_p, passages, passage_scale))
    ):
        all_ref[side] = scale * (grad - values * jnp.sum(grad * values, -1, keepdims=True))
        for row in range(own):
            grad_ref[side * own + row] = all_ref[side, pl.ds(me[0] * own + row, 1), :]


def loss_and_grads(queries, passages, source, positive, me, own):
    count = queries.shape[0]
    vmem = pl.BlockSpec(memory_space=pltpu.VMEM)
    return pl.pallas_call(
        loss_kernel,
        in_specs=[pl.BlockSpec(memory_space=pltpu.SMEM)] + [vmem] * 4,
        out_shape=[
            jax.ShapeDtypeStruct((1, 1), F32),
            jax.ShapeDtypeStruct((2 * own, 1, D), F32),
        ],
        scratch_shapes=[pltpu.VMEM((2, count, D), F32)],
        cost_estimate=CHEAP,
        compiler_params=pltpu.CompilerParams(vmem_limit_bytes=32 * MIB),
        name="loss",
    )(me[None], queries, passages, source.reshape(1, count), positive.reshape(count, 1))


def everyone(values):
    devices = lax.axis_size(AXES)
    copies = jnp.broadcast_to(values[None], (devices,) + values.shape)
    return lax.all_to_all(copies, AXES, 0, 0, tiled=True)


def other_core(values):
    return lax.ppermute(values, "core", [(0, 1), (1, 0)])


def tie(anchor, *values):
    return lax.optimization_barrier((anchor,) + values)


PLANE = ("x", "y")


def partner(index, shift, count):
    return (index + shift) % count if count & (count - 1) else index ^ shift


def partners_of(axes):
    count, me = lax.axis_size(axes), lax.axis_index(axes).astype(jnp.int32)
    return jnp.stack([jnp.int32(0) + partner(me, shift, count) for shift in range(count)])


def spread(values, axes):
    count = lax.axis_size(axes)
    return [values] + [
        lax.ppermute(values, axes, [(i, partner(i, shift, count)) for i in range(count)])
        for shift in range(1, count)
    ]


def trade(parts, axes):
    count = lax.axis_size(axes)
    return [parts[0]] + [
        lax.ppermute(parts[shift], axes, [(i, partner(i, shift, count)) for i in range(count)])
        for shift in range(1, count)
    ]


def finish_kernel(counts, table_squares, *refs):
    inputs, outputs = refs[: sum(counts)], refs[sum(counts) :]
    place_ref, qkv_ref, proj_ref, inner_ref, outer_ref, squares_ref = outputs
    totals, first = [], 0
    for count in counts:
        total = inputs[first][...]
        for more in inputs[first + 1 : first + count]:
            total = total + more[...].astype(F32)
        totals.append(total)
        first += count
    outer, inner, packed = totals
    pieces, rows = outer.shape[:2]
    squares = table_squares[...]
    for piece in range(pieces):
        outer_ref[piece * rows : (piece + 1) * rows] = outer[piece]
        inner_ref[:, piece * D : (piece + 1) * D] = inner[piece]
    for piece in range(3):
        qkv_ref[:, piece * D : (piece + 1) * D] = packed[piece]
    proj_ref[...] = inner[pieces]
    place_ref[...] = packed[3, : place_ref.shape[0]]
    for total in totals:
        squares = squares + jnp.sum(jnp.sum(total * total, 0), keepdims=True)
    squares_ref[...] = jnp.broadcast_to(squares[None], squares_ref.shape)


def finish(table_squares, outer, inner, packed, place_rows, devices):
    pieces, rows = outer[0].shape[:2]
    parts = (outer, inner, packed)
    return pl.pallas_call(
        functools.partial(finish_kernel, [len(part) for part in parts]),
        out_shape=[
            shape(place_rows, D, F32), shape(rows, 3 * D, F32), shape(rows, D, F32),
            shape(rows, pieces * D, F32), shape(pieces * rows, D, F32),
            jax.ShapeDtypeStruct((devices, 1, LANES), F32),
        ],
        cost_estimate=CHEAP,
        compiler_params=pltpu.CompilerParams(vmem_limit_bytes=60 * MIB),
        name="finish",
    )(table_squares, *outer, *inner, *packed)


def update_kernel(squares, *refs):
    count = 7
    gradients, masters, firsts, seconds = (refs[part * count : (part + 1) * count] for part in range(4))
    outputs, norm_ref = refs[4 * count : 7 * count], refs[7 * count]
    norm = jnp.sqrt(jnp.sum(squares[...][:, 0, :1], 0, keepdims=True))
    factor = jnp.minimum(1.0, CLIP_LIMIT / (norm + 1e-06))
    norm_ref[...] = norm

    def update(index):
        rate, decay = (VECTOR_RATE, 0.0) if index == count - 1 else (LEARN_RATE, WEIGHT_DECAY)
        clipped = gradients[index][...] * factor
        first = BETA_FIRST * firsts[index][...] + (1.0 - BETA_FIRST) * clipped
        second = BETA_SECOND * seconds[index][...] + (1.0 - BETA_SECOND) * clipped * clipped
        ratio = (
            first
            * (1.0 / (1.0 - BETA_FIRST**STEP))
            / (jnp.sqrt(second * (1.0 / (1.0 - BETA_SECOND**STEP))) + EPSILON)
        )
        master = masters[index][...]
        outputs[index][...] = master - rate * (ratio + decay * master)
        outputs[count + index][...] = first
        outputs[2 * count + index][...] = second

    update(0)

    @pl.when(pl.program_id(0) == 0)
    def _():
        for index in range(1, count):
            update(index)


def update_all(squares, gradients, masters, firsts, seconds):
    owned = masters[0].shape[0]
    block = max(size for size in range(8, 241, 8) if owned % size == 0)
    specs = [pl.BlockSpec((block, D), lambda i: (i, 0))]
    specs += [fixed(master.shape) for master in masters[1:]]
    return call(
        update_kernel, "update", (owned // block,),
        [fixed(squares.shape)] + specs * 4,
        specs * 3 + [fixed((1, 1))],
        [jax.ShapeDtypeStruct(master.shape, F32) for master in masters] * 3 + [shape(1, 1, F32)],
    )(squares, *gradients, *masters, *firsts, *seconds)


def per_device(query_ids, query_mask, passage_ids, passage_mask, source, positive, *weights):
    masters, firsts, seconds = weights[:7], weights[7:14], weights[14:]
    table, positions, w_qkv, w_o, w_in, w_out, vectors = masters
    sizes = tuple(lax.axis_size(name) for name in AXES)
    devices = lax.axis_size(AXES)
    pair_rows, length = query_ids.shape
    sequences = 2 * pair_rows
    tokens = sequences * length
    owned, rows = table.shape[0], w_qkv.shape[0]
    me = lax.axis_index(AXES)

    place_rows = positions.shape[0]
    vector_size = vectors.shape[0] * vectors.shape[1]
    vector_rows_used = -(-vector_size // D)
    vector_flat = jnp.pad(vectors.reshape(-1), (0, vector_rows_used * D - vector_size))
    units = w_in.shape[1]
    pieces = units // D
    core = lax.axis_index("core").astype(jnp.int32)[None]
    extents = (sizes[0],) + sizes[2:]
    in_plane, in_depth = partners_of(PLANE), partners_of("z")
    own_pieces = pieces_of(
        w_qkv, w_o, positions, vector_flat.reshape(vector_rows_used, D), w_in, w_out
    )
    column = lax.all_gather(own_pieces, "z", axis=0, tiled=True).reshape((sizes[2],) + own_pieces.shape)

    room = min(LANES - 1, max(16, round_up(5 * tokens // (4 * devices), 8)))
    query_ids, _ = tie(query_ids, own_pieces)
    slot_column, slot_row, rank, fresh, wants = plan_of(query_ids, passage_ids, owned, room, devices)
    swap = lambda values: lax.all_to_all(values, AXES, 0, 0, tiled=True)
    token_mask = jnp.concatenate([query_mask, passage_mask]).astype(F32)
    mask_row = token_mask[:, None, :]
    share = (token_mask / jnp.sum(token_mask, 1, keepdims=True)).reshape(tokens, 1)
    asked = swap(wants)
    zeros = jnp.zeros((tokens, D), F32)
    asked, mask_row, share, zeros = tie(asked, mask_row, share, zeros)
    chosen, found = lookup(asked, table, room)
    column, _ = tie(column, found)
    found = swap(found)
    plane = spread(column[:, :5], PLANE)
    pair_plane = spread(column[:, 5:], PLANE)
    plane_other = [other_core(part) for part in plane]
    (gathered,) = assemble("assemble", plane, plane_other, core, in_plane, extents, 5)

    turns = jnp.max(asked[:, LANES - 1]) // (room - 1) + 1
    slots = jnp.arange(devices * room, dtype=jnp.int32)
    ids = jnp.concatenate([query_ids, passage_ids]).reshape(-1)

    def turn_of(turn):
        spot = rank[0] - turn * (room - 1)
        slot = jnp.where((spot >= 0) & (spot < room - 1), ids // owned * room + spot, -1)
        match = (slots[:, None] == slot[None, :]) & (fresh > 0)
        wants = jnp.sum(jnp.where(match, ids % owned + 1, 0), 1).reshape(devices, room)
        return slot, swap(jnp.pad(wants, ((0, 0), (0, LANES - room))))

    def fetch_more(state):
        turn, values = state
        slot, asked = turn_of(turn)
        found = swap(lookup(asked, table, room)[1])
        return turn + 1, values + matmul((slot[:, None] == slots[None, :]).astype(BF16), found)

    _, looked_up = lax.while_loop(
        lambda state: state[0] < turns, fetch_more, (jnp.int32(1), zeros)
    )

    vec = vec_of(gathered, vectors.shape[0], vectors.shape[1], place_rows, rows)
    normal_zero, scale_zero, low_zero, packed = enter(
        slot_column, found, looked_up, vec, gathered, length, place_rows, rows
    )
    context, log_total = attend(packed, mask_row, sequences, length)
    context, *pair_plane = tie(context, *pair_plane)
    pair_other = [other_core(part) for part in pair_plane]
    inner_full, outer_full = assemble(
        "assemble_pair", pair_plane, pair_other, core, in_plane, extents, pieces, pieces
    )
    normal_one, scale_one, low_one, activated, slope, normal_two, scale_two, pooled = layer(
        normal_zero, context, share, vec, gathered, inner_full, outer_full, length
    )

    shared = everyone(pooled[:, 0]).reshape(devices, 2, pair_rows, D)
    loss, grad_pooled = loss_and_grads(
        shared[:, 0].reshape(-1, D), shared[:, 1].reshape(-1, D), source, positive,
        me.astype(jnp.int32), pair_rows,
    )

    by_plane = lambda values: values.reshape((-1,) + values.shape[2:])
    outer_kept, outer_sent = outer_grad(
        activated, grad_pooled, share, normal_two, scale_two, vec, core, extents, rows
    )
    outer_came = other_core(outer_sent)
    outer_parts = split("split_outer", [by_plane(outer_kept), by_plane(outer_came)], in_plane)
    outer_plane = trade(outer_parts, PLANE)
    slope, *_ = tie(slope, *outer_parts)
    grad_inner, grad_mixed, attended, grad_context, sums = layer_back(
        grad_pooled, share, normal_two, scale_two, slope, normal_one, scale_one, vec,
        gathered, inner_full, outer_full, length,
    )
    grad_inner, attended, *outer_plane = tie(grad_inner, attended, *outer_plane)
    outer_parts = fold("fold_outer", outer_plane, in_depth)
    outer_depth = trade(outer_parts, "z")
    grad_inner, attended, *_ = tie(grad_inner, attended, *outer_parts)
    inner_kept, inner_sent = weight_grad(
        "grad_inner", [(low_one, grad_inner), (context, attended)], core, extents
    )
    inner_kept, inner_sent, *outer_depth = tie(inner_kept, inner_sent, *outer_depth)
    inner_came = other_core(inner_sent)
    inner_parts = split("split_inner", [by_plane(inner_kept), by_plane(inner_came)], in_plane)
    inner_plane = trade(inner_parts, PLANE)
    grad_context, *_ = tie(grad_context, *inner_parts)
    grad_packed = attend_back(packed, mask_row, grad_context, log_total, sequences, length)
    grad_packed, *inner_plane = tie(grad_packed, *inner_plane)
    inner_parts = fold("fold_inner", inner_plane, in_depth)
    grad_packed, *inner_parts = tie(grad_packed, *inner_parts)
    inner_depth = trade(inner_parts, "z")
    low_input, grad_position, end_sums = leave(
        grad_packed, grad_mixed, normal_zero, scale_zero, vec, gathered, length, place_rows, rows
    )
    low_input, grad_position, end_sums, *inner_depth = tie(
        low_input, grad_position, end_sums, *inner_depth
    )

    grad_vectors = jnp.concatenate(
        [end_sums[2:4], sums[pieces + 5 : pieces + 6], sums[:pieces]]
        + [sums[pieces : pieces + 1], end_sums[:2], sums[pieces + 1 : pieces + 5]]
    )
    vector_pieces = grad_vectors.reshape(-1, devices, vectors.shape[1]).transpose(1, 0, 2)
    vector_pieces = vector_pieces.reshape(devices, -1)
    vector_high = lax.reduce_precision(vector_pieces, 8, 7)
    vector_pieces = jnp.concatenate([vector_high, vector_pieces - vector_high], 1)
    vector_pieces = jnp.pad(vector_pieces, ((0, 0), (0, D - 2 * vector_size))).astype(BF16)

    def give_more(state):
        turn, values = state
        slot, asked = turn_of(turn)
        given = swap(give_rows(slot[None], low_input, jnp.zeros_like(vector_pieces), room))
        return turn + 1, values + take_rows(lookup(asked, table, room)[0], given)

    summed = give_rows(slot_row, low_input, vector_pieces, room)
    given = swap(summed)
    low_zero, _ = tie(low_zero, summed)

    grad_position = jnp.pad(grad_position, ((0, devices - grad_position.shape[0]), (0, 0), (0, 0)))
    grad_position = grad_position.reshape(sizes + (rows, D))
    packed_kept, packed_sent = weight_grad(
        "grad_packed", [(low_zero, grad_packed)], core, extents, grad_position
    )
    packed_came = other_core(packed_sent)
    packed_plane = trade(split("split_packed", [by_plane(packed_kept), by_plane(packed_came)], in_plane), PLANE)
    _, table_grad = lax.while_loop(
        lambda state: state[0] < turns, give_more, (jnp.int32(1), take_rows(chosen, given))
    )
    sum_vectors = jnp.sum(
        given.reshape(devices, room, D)[:, room - 1, : 2 * vector_size].astype(F32), 0
    )
    sum_vectors = (sum_vectors[:vector_size] + sum_vectors[vector_size:]).reshape(vectors.shape)
    squares = jnp.sum(table_grad * table_grad) + jnp.sum(sum_vectors * sum_vectors)
    squares, *packed_plane = tie(squares, *packed_plane)
    packed_depth = trade(fold("fold_packed", packed_plane, in_depth), "z")
    *small_grads, squares = finish(
        squares.reshape(1, 1), outer_depth, inner_depth, packed_depth, place_rows, devices
    )
    squares = lax.all_to_all(squares, AXES, 0, 0, tiled=True)
    *new, grad_norm = update_all(
        squares, (table_grad, *small_grads, sum_vectors), masters, firsts, seconds
    )
    return (*new, loss[0, 0], grad_norm[0, 0])


def solution(mesh):
    outer, dp = mesh.shape["outer"], mesh.shape["dp"]
    x = outer // 2
    y = x if dp % x == 0 else 1
    fine = Mesh(np.asarray(mesh.devices).reshape(x, 2, dp // y, y), AXES)
    by_row, by_column, whole = P(AXES, None), P(None, AXES), P()
    seven = (by_row,) * 6 + (by_column,)
    return jax.shard_map(
        per_device,
        mesh=fine,
        in_specs=(by_row,) * 4 + (whole,) * 2 + seven * 3,
        out_specs=seven * 3 + (whole, whole),
        check_vma=False,
    )
```

time: 2430 us -> 480 us (0.20)
  waiting for transfers between devices: 1420 us -> 139 us
  blocking collectives: 298 us -> 0 us
  matrix products: 286 us -> 0 us
  other arithmetic: 242 us -> 7.88 us
  Pallas kernels: 0 us -> 210 us
  local copies, waits for them, and re-layouts: 109 us -> 32.7 us
  starting transfers between devices: 0.96 us -> 65.8 us
  between operations: 51.8 us -> 18.3 us
    reduce_scatter x6 -> x0, waiting for transfers between devices: 1130 us -> none  [the longest x1 785 us: per_device(): lax.psum_scatter(jnp.zeros((count, model_width), jnp.float32).at[jnp.wher...]
    dot_general x49 -> x0, matrix products: 262 us -> none  [the longest x28 186 us: matmul(): return jnp.dot(left, right, preferred_element_type=jnp.float32)]
    all_gather x3 -> x0, blocking collectives: 217 us -> none  [the longest x1 77.3 us: per_device(): lax.all_gather(positions.astype(jnp.bfloat16), ('outer', 'dp'), axis=0, t...]
    pallas_call x0 -> x26, Pallas kernels: none -> 210 us  [the longest x1 25 us: attend_back(): call(attend_back_kernel, 'attend_back', (sequences, PARTS), inputs + [pla...]
    all_gather x5 -> x1, waiting for transfers between devices: 177 us -> 6.58 us  [per_device(): lax.all_gather(own_pieces, 'z', axis=0, tiled=True)]
    scatter-add x1 -> x0, other arithmetic: 131 us -> none  [per_device(): table_grad = lax.psum_scatter(jnp.zeros((count, model_width), jnp.float32...]
    unnamed x13 -> x1, waiting for transfers between devices: 113 us -> 0.02 us
    ppermute x0 -> x35, waiting for transfers between devices: none -> 86.2 us  [the longest x6 43.9 us: spread(): lax.ppermute(values, axes, [(i, partner(i, shift, count)) for i in range(...]
  transfers between devices with their start and end apart: 12 -> 41, of which waited for: 8 -> 21; matrix products, arithmetic and copies ran while one was open for 17% -> 3% of each run, Pallas kernels for 0% -> 28%
where the time goes in v1:
time: 480 us; the launch traced here: 474 us
  Pallas kernels  210 us (44%)
  waiting for transfers between devices  139 us (29%)
  starting transfers between devices  65.8 us (14%)
  local copies, waits for them, and re-layouts  32.7 us (7%)
  between operations  18.3 us (4%)
  other arithmetic  7.88 us (2%)
    ppermute x6, waiting for transfers between devices, spread(): lax.ppermute(values, axes, [(i, partner(i, shift, count)) for i in range(...  43.9 us
    all_to_all x3, waiting for transfers between devices, per_device(): swap = lambda values: lax.all_to_all(values, AXES, 0, 0, tiled=True)  31.1 us
    pallas_call x1, Pallas kernels, attend_back(): call(attend_back_kernel, 'attend_back', (sequences, PARTS), inputs + [pla...  25 us
    pallas_call x1, Pallas kernels, layer(): call(functools.partial(layer_kernel, cycle, pieces), 'layer', (tokens //...  24.7 us
    ppermute x18, starting transfers between devices, trade(): lax.ppermute(parts[shift], axes, [(i, partner(i, shift, count)) for i in...  23.8 us
    pallas_call x1, Pallas kernels, layer_back(): call(functools.partial(layer_back_kernel, pieces), 'layer_back', (tokens...  23.4 us
    unnamed x112, local copies, waits for them, and re-layouts  22.5 us
    ppermute x11, waiting for transfers between devices, other_core(): return lax.ppermute(values, 'core', [(0, 1), (1, 0)])  21.5 us
  transfers between devices with their start and end apart: 41, of which 21 were waited for; matrix products, arithmetic and copies ran while one was open for 3% of the time, Pallas kernels for 28%

profile of v1, /device:TPU:0, one launch (start us, length us, event | category | flops | bytes accessed | tf_op | source)
XLA Modules:
  0.0 473.6 jit_solution(14648170899156909455)
XLA Ops:
  12.1 4.1 plan.1
  18.6 7.3 %all-to-all-start.4 = ((s32[32,1,128]{2,1,0:T(1,128)}), s32[32,1,128]{2,1,0:T(1,128)S(1)}, u32[]{:S(2)}, u32[]{:S(2)}) async-start(s32[32,1,128]{2,1,0:T(1,128)} %bitcast.1), calls=%async_computation.4 | async-start | bytes 32768 | tf_op jit(solution)/shard_map/all_to_all | solution.py:935
  26.6 6.4 %all-to-all-done.4 = s32[32,1,128]{2,1,0:T(1,128)S(1)} async-done(((s32[32,1,128]{2,1,0:T(1,128)}), s32[32,1,128]{2,1,0:T(1,128)S(1)}, u32[]{:S(2)}, u32[]{:S(2)}) %all-to-all-start.4) | async-done | bytes 16416 | tf_op jit(solution)/shard_map/all_to_all | solution.py:935
  35.7 6.0 %lookup.9 = (bf16[1280,960]{1,0:T(8,128)(2,1)}, bf16[1280,768]{1,0:T(8,128)(2,1)}) custom-call(s32[32,128]{1,0:T(8,128)} %bitcast.156, f32[960,768]{1,0:T(8,128)} %refs_7_.1), custom_call_target="tpu_custom_call" | custom-call | flops 1 | bytes 1 | tf_op jit(solution)/shard_map/lookup/pallas_call | solution.py:224
  43.8 9.6 %all-to-all-start.5 = ((bf16[32,40,768]{2,1,0:T(8,128)(2,1)}), bf16[32,40,768]{2,1,0:T(8,128)(2,1)}, u32[]{:S(2)}, u32[]{:S(2)}) async-start(bf16[32,40,768]{2,1,0:T(8,128)(2,1)} %bitcast.139), calls=%async_computation.5 | async-start | bytes 3932160 | tf_op jit(solution)/shard_map/all_to_all | solution.py:935
  53.5 6.6 %all-gather.2.cloned.1.call-done = bf16[52,24,768]{2,1,0:T(8,128)(2,1)} async-done(((bf16[13,24,768]{2,1,0:T(8,128)(2,1)}), bf16[52,24,768]{2,1,0:T(8,128)(2,1)}) %all-gather.2.cloned.1.call-update) | async-done | bytes 1916944 | tf_op jit(solution)/shard_map/all_gather | solution.py:930
  64.8 27.7 %collective-permute-done.refs_1_ = bf16[4,5,24,768]{3,2,1,0:T(8,128)(2,1)S(1)} collective-permute-done((bf16[4,5,24,768]{3,2,1,0:T(8,128)(2,1)S(1)}, bf16[4,5,24,768]{3,2,1,0:T(8,128)(2,1)S(1)}, u32[]{:S(2)}, u32[]{:S(2)}) %collective-permute-start) | collective-permute-done | bytes 737312 | tf_op jit(solution)/shard_map/ppermute | solution.py:809
  96.7 13.1 %collective-permute-done.2.refs_3_ = bf16[4,5,24,768]{3,2,1,0:T(8,128)(2,1)S(1)} collective-permute-done((bf16[4,5,24,768]{3,2,1,0:T(8,128)(2,1)S(1)}, bf16[4,5,24,768]{3,2,1,0:T(8,128)(2,1)S(1)}, u32[]{:S(2)}, u32[]{:S(2)}) %collective-permute-start.2) | collective-permute-done | bytes 737312 | tf_op jit(solution)/shard_map/ppermute | solution.py:809
  115.4 7.1 %assemble.1 = bf16[2,2,4,2,24,3840]{5,4,3,2,1,0:T(8,128)(2,1)} custom-call(s32[1]{0:T(128)} %bitcast.7.core, s32[4]{0:T(128)} %pad_add_fusion.1.in_plane.partners, bf16[4,5,24,768]{3,2,1,0:T(8,128)(2,1)} %copy-done.35, bf16[4,5,24,768]{3,2,1,0:T(8,128)(2,1)} %copy-done.37, bf16[4,5,24,768]{3,2,1,0:T(8,128)(2,1)} %copy-done.38, ...), custom_call_target="tpu_custom_call" | custom-call | flops 1 | bytes 1 | tf_op jit(solution)/shard_map/assemble/pallas_call | solution.py:602
  126.2 12.9 %enter.1 = (f32[1024,768]{1,0:T(8,128)}, f32[1024,1]{1,0:T(8,128)}, bf16[1024,768]{1,0:T(8,128)(2,1)}, bf16[1024,2304]{1,0:T(8,128)(2,1)}) custom-call(s32[1024,1]{1,0:T(8,128)} %copy-done.22, bf16[1280,768]{1,0:T(8,128)(2,1)} %bitcast.6.found_ref, f32[1024,768]{1,0:T(8,128)S(1)} %copy-done.33, bf16[768,3840]{1,0:T(8,128)(2,1)} %bitcast.112, ...), custom_call_target="tpu_custom_call" | custom-call | flops 1 | bytes 1 | tf_op jit(solution)/shard_map/enter/pallas_call | solution.py:264
  141.4 13.3 %attend.1 = (bf16[1024,768]{1,0:T(8,128)(2,1)S(1)}, f32[2,1024,128]{2,1,0:T(8,128)S(1)}) custom-call(f32[2,1,512]{2,1,0:T(1,128)S(1)} %add_convert_fusion.mask_ref, bf16[1024,2304]{1,0:T(8,128)(2,1)S(1)} %copy-done.1, bf16[1024,2304]{1,0:T(8,128)(2,1)S(1)} %copy-done.1, bf16[1024,2304]{1,0:T(8,128)(2,1)S(1)} %copy-done.1), custom_call_target="tpu_custom_call" | custom-call | flops 1 | bytes 1 | tf_op jit(solution)/shard_map/attend/pallas_call | solution.py:699
  167.2 7.8 %assemble_pair.1 = (bf16[2,2,4,2,24,3072]{5,4,3,2,1,0:T(8,128)(2,1)}, bf16[2,2,4,2,4,24,768]{6,5,4,3,2,1,0:T(8,128)(2,1)}) custom-call(s32[1]{0:T(128)} %bitcast.7.core, s32[4]{0:T(128)} %pad_add_fusion.1.in_plane.partners, bf16[4,8,24,768]{3,2,1,0:T(8,128)(2,1)} %slice.59.refs_0_.refs_1_, bf16[4,8,24,768]{3,2,1,0:T(8,128)(2,1)} %slice.59.refs_0_.refs_1_, ...), custom_call_target="tpu_custom_call" | custom-call | flops 1 | bytes 1 | tf_op jit(solution)/shard_map/assemble_pair/pallas_call | solution.py:602
  175.0 24.7 %layer.1 = (f32[1024,768]{1,0:T(8,128)}, f32[1024,1]{1,0:T(8,128)}, bf16[1024,768]{1,0:T(8,128)(2,1)}, bf16[1024,3072]{1,0:T(8,128)(2,1)}, f32[1024,3072]{1,0:T(...) custom-call(f32[1024,768]{1,0:T(8,128)} %get-tuple-element.423.refs_0_.normal, ...), custom_call_target="tpu_custom_call" | custom-call | flops 1 | bytes 1 | tf_op jit(solution)/shard_map/layer/pallas_call | solution.py:306
  201.2 6.7 %all-to-all-start.6 = ((f32[32,2,768]{2,1,0:T(2,128)}), f32[32,2,768]{2,1,0:T(2,128)S(1)}, u32[]{:S(2)}, u32[]{:S(2)}) async-start(f32[32,2,768]{2,1,0:T(2,128)} %broadcast_in_dim.61), calls=%async_computation.6 | async-start | bytes 393216 | tf_op jit(solution)/shard_map/all_to_all | solution.py:783
  208.0 8.4 %all-to-all-done.6 = f32[32,2,768]{2,1,0:T(2,128)S(1)} async-done(((f32[32,2,768]{2,1,0:T(2,128)}), f32[32,2,768]{2,1,0:T(2,128)S(1)}, u32[]{:S(2)}, u32[]{:S(2)}) %all-to-all-start.6) | async-done | bytes 196640 | tf_op jit(solution)/shard_map/all_to_all | solution.py:783
  225.6 8.3 %grad_outer.1 = (f32[2,2,4,4,24,768]{5,4,3,2,1,0:T(8,128)S(1)}, bf16[2,2,4,4,24,768]{5,4,3,2,1,0:T(8,128)(2,1)S(1)}) custom-call(s32[1]{0:T(128)} %bitcast.7.core, bf16[1024,3072]{1,0:T(8,128)(2,1)S(1)} %copy-done.10, f32[2,1,768]{2,1,0:T(1,128)S(1)} %get-tuple-element.434.grad_pooled.refs_0_, f32[1024,1]{1,0:T(8,128)S(1)} %copy-done.6, ...), custom_call_target="tpu_custom_call" | custom-call | flops 1 | bytes 1 | tf_op jit(solution)/shard_map/grad_outer/pallas_call | solution.py:512
  234.1 4.4 collective-permute-done.14
  244.6 23.4 %layer_back.1 = (bf16[1024,3072]{1,0:T(8,128)(2,1)}, f32[1024,768]{1,0:T(8,128)}, bf16[1024,768]{1,0:T(8,128)(2,1)}, bf16[1024,768]{1,0:T(8,128)(2,1)}, f32[16,768]{1,0:T(8,128)}) custom-call(f32[2,1,768]{2,1,0:T(1,128)} %copy-done.26, f32[1024,1]{1,0:T(8,128)} %copy.65.refs_2_.share.refs_1_, f32[1024,768]{1,0:T(8,128)} %get-tuple-element.435.normal.refs_2_, ...), custom_call_target="tpu_custom_call" | custom-call | flops 1 | bytes 1 | tf_op jit(solution)/shard_map/layer_back/pallas_call | solution.py:357
  279.0 10.0 %grad_inner.1 = (f32[2,2,5,4,24,768]{5,4,3,2,1,0:T(8,128)S(1)}, bf16[2,2,5,4,24,768]{5,4,3,2,1,0:T(8,128)(2,1)S(1)}) custom-call(s32[1]{0:T(128)} %bitcast.7.core, bf16[1024,768]{1,0:T(8,128)(2,1)S(1)} %copy-done.17, bf16[1024,3072]{1,0:T(8,128)(2,1)} %get-tuple-element.462.refs_1_, bf16[1024,768]{1,0:T(8,128)(2,1)S(1)} %copy-done.9, ...), custom_call_target="tpu_custom_call" | custom-call | flops 1 | bytes 1 | tf_op jit(solution)/shard_map/grad_inner/pallas_call | solution.py:469
  289.2 5.4 %collective-permute-done.21 = bf16[2,2,5,4,24,768]{5,4,3,2,1,0:T(8,128)(2,1)S(1)} collective-permute-done((bf16[2,2,5,4,24,768]{5,4,3,2,1,0:T(8,128)(2,1)S(1)}, bf16[2,2,5,4,24,768]{5,4,3,2,1,0:T(8,128)(2,1)S(1)}, u32[]{:S(2)}, u32[]{:S(2)}) %collective-permute-start.21) | collective-permute-done | bytes 2949152 | tf_op jit(solution)/shard_map/ppermute | solution.py:787
  301.4 25.0 %attend_back.1.packed.refs_1_ = bf16[1024,2304]{1,0:T(8,128)(2,1)S(1)} custom-call(f32[2,1,512]{2,1,0:T(1,128)S(1)} %add_convert_fusion.mask_ref, bf16[1024,2304]{1,0:T(8,128)(2,1)S(1)} %bitcast.102, bf16[1024,2304]{1,0:T(8,128)(2,1)S(1)} %bitcast.102, bf16[1024,2304]{1,0:T(8,128)(2,1)S(1)} %bitcast.102, bf16[1024,768]{1,0:T(8,128)(2,1)S(1)} %copy-done.18, ...), custom_call_target="tpu_custom_call" | custom-call | flops 1 | bytes 1 | tf_op jit(solution)/shard_map/attend_back/pallas_call | solution.py:707
  326.5 6.9 %collective-permute-done.24.refs_3_ = bf16[5,4,24,768]{3,2,1,0:T(8,128)(2,1)S(1)} collective-permute-done((bf16[5,4,24,768]{3,2,1,0:T(8,128)(2,1)S(1)}, bf16[5,4,24,768]{3,2,1,0:T(8,128)(2,1)S(1)}, u32[]{:S(2)}, u32[]{:S(2)}) %collective-permute-start.24) | collective-permute-done | bytes 737312 | tf_op jit(solution)/shard_map/ppermute | solution.py:817
  338.9 8.9 %leave.1 = (bf16[1024,768]{1,0:T(8,128)(2,1)S(1)}, f32[32,24,768]{2,1,0:T(8,128)S(1)}, f32[8,768]{1,0:T(8,128)S(1)}) custom-call(bf16[1024,2304]{1,0:T(8,128)(2,1)S(1)} %attend_back.1.packed.refs_1_, f32[1024,768]{1,0:T(8,128)S(1)} %copy-done.11, f32[1024,768]{1,0:T(8,128)S(1)} %copy-done.5, f32[1024,1]{1,0:T(8,128)S(1)} %copy-done.21, ...), custom_call_target="tpu_custom_call" | custom-call | flops 1 | bytes 1 | tf_op jit(solution)/shard_map/leave/pallas_call | solution.py:401
  356.8 4.3 all-to-all-start.7
  361.1 9.7 %grad_packed.1 = (f32[2,2,4,4,24,768]{5,4,3,2,1,0:T(8,128)}, bf16[2,2,4,4,24,768]{5,4,3,2,1,0:T(8,128)(2,1)}) custom-call(s32[1]{0:T(128)} %bitcast.7.core, bf16[1024,768]{1,0:T(8,128)(2,1)} %get-tuple-element.498.refs_0_, bf16[1024,2304]{1,0:T(8,128)(2,1)} %copy-done.3, f32[2,2,4,2,24,768]{5,4,3,2,1,0:T(8,128)} %bitcast.109), custom_call_target="tpu_custom_call" | custom-call | flops 1 | bytes 1 | tf_op jit(solution)/shard_map/grad_packed/pallas_call | solution.py:469
  371.1 4.5 collective-permute-done.28
  375.7 5.1 %split_packed.1 = (f32[4,4,24,768]{3,2,1,0:T(8,128)}, bf16[4,4,24,768]{3,2,1,0:T(8,128)(2,1)}, bf16[4,4,24,768]{3,2,1,0:T(8,128)(2,1)}, bf16[4,4,24,768]{3,2,1,0:T(8,128)(2,1)}) custom-call(s32[4]{0:T(128)} %pad_add_fusion.1.in_plane.partners, f32[4,4,4,24,768]{4,3,2,1,0:T(8,128)} %bitcast.138, bf16[4,4,4,24,768]{4,3,2,1,0:T(8,128)(2,1)} %bitcast.35.refs_1_), custom_call_target="tpu_custom_call" | custom-call | flops 1 | bytes 1 | tf_op jit(solution)/shard_map/split_packed/pallas_call | solution.py:545
  384.2 24.8 %all-to-all-done.7 = bf16[32,40,768]{2,1,0:T(8,128)(2,1)S(1)} async-done(((bf16[32,40,768]{2,1,0:T(8,128)(2,1)}), bf16[32,40,768]{2,1,0:T(8,128)(2,1)S(1)}, u32[]{:S(2)}, u32[]{:S(2)}) %all-to-all-start.7) | async-done | bytes 1966112 | tf_op jit(solution)/shard_map/all_to_all | solution.py:935
  430.4 6.5 %collective-permute-done.33.refs_10_ = bf16[4,24,768]{2,1,0:T(8,128)(2,1)S(1)} collective-permute-done((bf16[4,24,768]{2,1,0:T(8,128)(2,1)S(1)}, bf16[4,24,768]{2,1,0:T(8,128)(2,1)S(1)}, u32[]{:S(2)}, u32[]{:S(2)}) %collective-permute-start.33) | collective-permute-done | bytes 147488 | tf_op jit(solution)/shard_map/ppermute | solution.py:817
  440.5 5.1 %all-to-all-start.8 = ((f32[32,1,128]{2,1,0:T(1,128)}), f32[32,1,128]{2,1,0:T(1,128)S(1)}, u32[]{:S(2)}, u32[]{:S(2)}) async-start(f32[32,1,128]{2,1,0:T(1,128)} %get-tuple-element.523), calls=%async_computation.8 | async-start | bytes 32768 | tf_op jit(solution)/shard_map/all_to_all | solution.py:1067
  446.2 6.4 %all-to-all-done.8.squares = f32[32,1,128]{2,1,0:T(1,128)S(1)} async-done(((f32[32,1,128]{2,1,0:T(1,128)}), f32[32,1,128]{2,1,0:T(1,128)S(1)}, u32[]{:S(2)}, u32[]{:S(2)}) %all-to-all-start.8) | async-done | bytes 16416 | tf_op jit(solution)/shard_map/all_to_all | solution.py:1067
  453.2 13.4 %update.1 = (f32[960,768]{1,0:T(8,128)}, f32[16,768]{1,0:T(8,128)}, f32[24,2304]{1,0:T(8,128)}, f32[24,768]{1,0:T(8,128)}, f32[24,3072]{1,0:T(8,128)}, /*index=5...) custom-call(f32[32,1,128]{2,1,0:T(1,128)} %copy-done.52, ...), custom_call_target="tpu_custom_call" | custom-call | flops 1 | bytes 1 | tf_op jit(solution)/shard_map/update/pallas_call | solution.py:899
  (225 shorter events, 121.9 us)
Async XLA Ops:
  7.2 52.9 %all-gather.2.cloned.1.call-start = ((), (), s32[]{:S(2)}) async-start(), calls=%async_computation.9 | async-start | bytes 2396160 | tf_op jit(solution)/shard_map/all_gather | solution.py:930
  18.6 14.4 %all-to-all-start.4 = ((s32[32,1,128]{2,1,0:T(1,128)}), s32[32,1,128]{2,1,0:T(1,128)S(1)}, u32[]{:S(2)}, u32[]{:S(2)}) async-start(s32[32,1,128]{2,1,0:T(1,128)} %bitcast.1), calls=%async_computation.4 | async-start | bytes 32768 | tf_op jit(solution)/shard_map/all_to_all | solution.py:935
  43.8 82.3 %all-to-all-start.5 = ((bf16[32,40,768]{2,1,0:T(8,128)(2,1)}), bf16[32,40,768]{2,1,0:T(8,128)(2,1)}, u32[]{:S(2)}, u32[]{:S(2)}) async-start(bf16[32,40,768]{2,1,0:T(8,128)(2,1)} %bitcast.139), calls=%async_computation.5 | async-start | bytes 3932160 | tf_op jit(solution)/shard_map/all_to_all | solution.py:935
  61.2 31.3 %collective-permute-start = (bf16[4,5,24,768]{3,2,1,0:T(8,128)(2,1)S(1)}, bf16[4,5,24,768]{3,2,1,0:T(8,128)(2,1)S(1)}, u32[]{:S(2)}, u32[]{:S(2)}) collective-permute-start(bf16[4,5,24,768]{3,2,1,0:T(8,128)(2,1)S(1)} %slice.58.refs_0_), channel_id=1, source_target_pairs={{0,1},{1,0},{16,17},{17,16},{2,3},{3,2},{18,19},{19,18},{4,5},{5,4... | collective-permute-start | bytes 2211848 | tf_op jit(solution)/shard_map/ppermute | solution.py:809
  61.3 33.9 %collective-permute-start.1 = (bf16[4,5,24,768]{3,2,1,0:T(8,128)(2,1)S(1)}, bf16[4,5,24,768]{3,2,1,0:T(8,128)(2,1)S(1)}, u32[]{:S(2)}, u32[]{:S(2)}) collective-permute-start(bf16[4,5,24,768]{3,2,1,0:T(8,128)(2,1)S(1)} %slice.58.refs_0_), channel_id=1, source_target_pairs={{0,16},{1,17},{16,0},{17,1},{2,18},{3,19},{18,2},{19,3},{4,20},{5,... | collective-permute-start | bytes 2211848 | tf_op jit(solution)/shard_map/ppermute | solution.py:809
  63.7 46.0 %collective-permute-start.2 = (bf16[4,5,24,768]{3,2,1,0:T(8,128)(2,1)S(1)}, bf16[4,5,24,768]{3,2,1,0:T(8,128)(2,1)S(1)}, u32[]{:S(2)}, u32[]{:S(2)}) collective-permute-start(bf16[4,5,24,768]{3,2,1,0:T(8,128)(2,1)S(1)} %slice.58.refs_0_), channel_id=1, source_target_pairs={{0,17},{1,16},{16,1},{17,0},{2,19},{3,18},{18,3},{19,2},{4,21},{5,... | collective-permute-start | bytes 2211848 | tf_op jit(solution)/shard_map/ppermute | solution.py:809
  64.8 47.2 %collective-permute-start.3 = (bf16[4,5,24,768]{3,2,1,0:T(8,128)(2,1)S(1)}, bf16[4,5,24,768]{3,2,1,0:T(8,128)(2,1)S(1)}, u32[]{:S(2)}, u32[]{:S(2)}) collective-permute-start(bf16[4,5,24,768]{3,2,1,0:T(8,128)(2,1)S(1)} %slice.58.refs_0_), channel_id=1, source_target_pairs={{0,8},{8,0},{1,9},{9,1},{2,10},{10,2},{3,11},{11,3},{4,12},{12,4},... | collective-permute-start | bytes 2211848 | tf_op jit(solution)/shard_map/ppermute | solution.py:787
  92.5 19.5 %collective-permute-start.4 = (bf16[4,5,24,768]{3,2,1,0:T(8,128)(2,1)S(1)}, bf16[4,5,24,768]{3,2,1,0:T(8,128)(2,1)S(1)}, u32[]{:S(2)}, u32[]{:S(2)}) collective-permute-start(bf16[4,5,24,768]{3,2,1,0:T(8,128)(2,1)S(1)} %collective-permute-done.refs_1_), channel_id=1, source_target_pairs={{0,8},{8,0},{1,9},{9,1},{2,10},{10,2},{3,11},{11,3},{4,12},{12,4},... | collective-permute-start | bytes 2211848 | tf_op jit(solution)/shard_map/ppermute | solution.py:787
  95.2 60.7 %collective-permute-start.7 = (bf16[4,8,24,768]{3,2,1,0:T(8,128)(2,1)}, bf16[4,8,24,768]{3,2,1,0:T(8,128)(2,1)}, u32[]{:S(2)}, u32[]{:S(2)}) collective-permute-start(bf16[4,8,24,768]{3,2,1,0:T(8,128)(2,1)} %slice.59.refs_0_.refs_1_), channel_id=1, source_target_pairs={{0,1},{1,0},{16,17},{17,16},{2,3},{3,2},{18,19},{19,18},{4,5},{5,4... | collective-permute-start | bytes 3538952 | tf_op jit(solution)/shard_map/ppermute | solution.py:809
  95.2 60.7 %collective-permute-start.8 = (bf16[4,8,24,768]{3,2,1,0:T(8,128)(2,1)}, bf16[4,8,24,768]{3,2,1,0:T(8,128)(2,1)}, u32[]{:S(2)}, u32[]{:S(2)}) collective-permute-start(bf16[4,8,24,768]{3,2,1,0:T(8,128)(2,1)} %slice.59.refs_0_.refs_1_), channel_id=1, source_target_pairs={{0,16},{1,17},{16,0},{17,1},{2,18},{3,19},{18,2},{19,3},{4,20},{5,... | collective-permute-start | bytes 3538952 | tf_op jit(solution)/shard_map/ppermute | solution.py:809
  109.7 49.2 %collective-permute-start.9 = (bf16[4,8,24,768]{3,2,1,0:T(8,128)(2,1)}, bf16[4,8,24,768]{3,2,1,0:T(8,128)(2,1)}, u32[]{:S(2)}, u32[]{:S(2)}) collective-permute-start(bf16[4,8,24,768]{3,2,1,0:T(8,128)(2,1)} %slice.59.refs_0_.refs_1_), channel_id=1, source_target_pairs={{0,17},{1,16},{16,1},{17,0},{2,19},{3,18},{18,3},{19,2},{4,21},{5,... | collective-permute-start | bytes 3538952 | tf_op jit(solution)/shard_map/ppermute | solution.py:809
  159.5 7.7 %collective-permute-start.13 = (bf16[4,8,24,768]{3,2,1,0:T(8,128)(2,1)}, bf16[4,8,24,768]{3,2,1,0:T(8,128)(2,1)}, u32[]{:S(2)}, u32[]{:S(2)}) collective-permute-start(bf16[4,8,24,768]{3,2,1,0:T(8,128)(2,1)} %collective-permute-done.9.refs_6_.refs_7_), channel_id=1, source_target_pairs={{0,8},{8,0},{1,9},{9,1},{2,10},{10,2},{3,11},{11,3},{4,12},{12,4},... | collective-permute-start | bytes 3538952 | tf_op jit(solution)/shard_map/ppermute | solution.py:787
  201.2 15.2 %all-to-all-start.6 = ((f32[32,2,768]{2,1,0:T(2,128)}), f32[32,2,768]{2,1,0:T(2,128)S(1)}, u32[]{:S(2)}, u32[]{:S(2)}) async-start(f32[32,2,768]{2,1,0:T(2,128)} %broadcast_in_dim.61), calls=%async_computation.6 | async-start | bytes 393216 | tf_op jit(solution)/shard_map/all_to_all | solution.py:783
  241.0 27.0 %collective-permute-start.15 = (bf16[4,4,24,768]{3,2,1,0:T(8,128)(2,1)}, bf16[4,4,24,768]{3,2,1,0:T(8,128)(2,1)}, u32[]{:S(2)}, u32[]{:S(2)}) collective-permute-start(bf16[4,4,24,768]{3,2,1,0:T(8,128)(2,1)} %get-tuple-element.442), channel_id=1, source_target_pairs={{0,1},{1,0},{16,17},{17,16},{2,3},{3,2},{18,19},{19,18},{4,5},{5,4... | collective-permute-start | bytes 1769480 | tf_op jit(solution)/shard_map/ppermute | solution.py:817
  242.8 25.2 %collective-permute-start.16 = (bf16[4,4,24,768]{3,2,1,0:T(8,128)(2,1)}, bf16[4,4,24,768]{3,2,1,0:T(8,128)(2,1)}, u32[]{:S(2)}, u32[]{:S(2)}) collective-permute-start(bf16[4,4,24,768]{3,2,1,0:T(8,128)(2,1)} %get-tuple-element.443), channel_id=1, source_target_pairs={{0,16},{1,17},{16,0},{17,1},{2,18},{3,19},{18,2},{19,3},{4,20},{5,... | collective-permute-start | bytes 1769480 | tf_op jit(solution)/shard_map/ppermute | solution.py:817
  243.4 27.2 %collective-permute-start.17 = (bf16[4,4,24,768]{3,2,1,0:T(8,128)(2,1)}, bf16[4,4,24,768]{3,2,1,0:T(8,128)(2,1)}, u32[]{:S(2)}, u32[]{:S(2)}) collective-permute-start(bf16[4,4,24,768]{3,2,1,0:T(8,128)(2,1)} %get-tuple-element.444), channel_id=1, source_target_pairs={{0,17},{1,16},{16,1},{17,0},{2,19},{3,18},{18,3},{19,2},{4,21},{5,... | collective-permute-start | bytes 1769480 | tf_op jit(solution)/shard_map/ppermute | solution.py:817
  273.1 15.9 %collective-permute-start.18 = (bf16[4,24,768]{2,1,0:T(8,128)(2,1)S(1)}, bf16[4,24,768]{2,1,0:T(8,128)(2,1)S(1)}, u32[]{:S(2)}, u32[]{:S(2)}) collective-permute-start(bf16[4,24,768]{2,1,0:T(8,128)(2,1)S(1)} %get-tuple-element.459), channel_id=1, source_target_pairs={{0,2},{2,0},{4,6},{6,4},{1,3},{3,1},{5,7},{7,5},{8,10},{10,8},{12,... | collective-permute-start | bytes 442376 | tf_op jit(solution)/shard_map/ppermute | solution.py:817
  274.8 14.3 %collective-permute-start.19 = (bf16[4,24,768]{2,1,0:T(8,128)(2,1)S(1)}, bf16[4,24,768]{2,1,0:T(8,128)(2,1)S(1)}, u32[]{:S(2)}, u32[]{:S(2)}) collective-permute-start(bf16[4,24,768]{2,1,0:T(8,128)(2,1)S(1)} %get-tuple-element.460), channel_id=1, source_target_pairs={{0,4},{2,6},{4,0},{6,2},{1,5},{3,7},{5,1},{7,3},{8,12},{10,14},{12... | collective-permute-start | bytes 442376 | tf_op jit(solution)/shard_map/ppermute | solution.py:817
  275.5 13.6 %collective-permute-start.20 = (bf16[4,24,768]{2,1,0:T(8,128)(2,1)S(1)}, bf16[4,24,768]{2,1,0:T(8,128)(2,1)S(1)}, u32[]{:S(2)}, u32[]{:S(2)}) collective-permute-start(bf16[4,24,768]{2,1,0:T(8,128)(2,1)S(1)} %get-tuple-element.461), channel_id=1, source_target_pairs={{0,6},{2,4},{4,2},{6,0},{1,7},{3,5},{5,3},{7,1},{8,14},{10,12},{12... | collective-permute-start | bytes 442376 | tf_op jit(solution)/shard_map/ppermute | solution.py:817
  297.8 28.6 %collective-permute-start.22 = (bf16[5,4,24,768]{3,2,1,0:T(8,128)(2,1)}, bf16[5,4,24,768]{3,2,1,0:T(8,128)(2,1)S(1)}, u32[]{:S(2)}, u32[]{:S(2)}) collective-permute-start(bf16[5,4,24,768]{3,2,1,0:T(8,128)(2,1)} %get-tuple-element.469), channel_id=1, source_target_pairs={{0,1},{1,0},{16,17},{17,16},{2,3},{3,2},{18,19},{19,18},{4,5},{5,4... | collective-permute-start | bytes 2211848 | tf_op jit(solution)/shard_map/ppermute | solution.py:817
  299.5 26.9 %collective-permute-start.23 = (bf16[5,4,24,768]{3,2,1,0:T(8,128)(2,1)S(1)}, bf16[5,4,24,768]{3,2,1,0:T(8,128)(2,1)S(1)}, u32[]{:S(2)}, u32[]{:S(2)}) collective-permute-start(bf16[5,4,24,768]{3,2,1,0:T(8,128)(2,1)S(1)} %get-tuple-element.470), channel_id=1, source_target_pairs={{0,16},{1,17},{16,0},{17,1},{2,18},{3,19},{18,2},{19,3},{4,20},{5,... | collective-permute-start | bytes 2211848 | tf_op jit(solution)/shard_map/ppermute | solution.py:817
  300.1 33.2 %collective-permute-start.24 = (bf16[5,4,24,768]{3,2,1,0:T(8,128)(2,1)S(1)}, bf16[5,4,24,768]{3,2,1,0:T(8,128)(2,1)S(1)}, u32[]{:S(2)}, u32[]{:S(2)}) collective-permute-start(bf16[5,4,24,768]{3,2,1,0:T(8,128)(2,1)S(1)} %get-tuple-element.471), channel_id=1, source_target_pairs={{0,17},{1,16},{16,1},{17,0},{2,19},{3,18},{18,3},{19,2},{4,21},{5,... | collective-permute-start | bytes 2211848 | tf_op jit(solution)/shard_map/ppermute | solution.py:817
  334.4 14.8 %collective-permute-start.25 = (bf16[5,24,768]{2,1,0:T(8,128)(2,1)S(1)}, bf16[5,24,768]{2,1,0:T(8,128)(2,1)S(1)}, u32[]{:S(2)}, u32[]{:S(2)}) collective-permute-start(bf16[5,24,768]{2,1,0:T(8,128)(2,1)S(1)} %get-tuple-element.490), channel_id=1, source_target_pairs={{0,2},{2,0},{4,6},{6,4},{1,3},{3,1},{5,7},{7,5},{8,10},{10,8},{12,... | collective-permute-start | bytes 552968 | tf_op jit(solution)/shard_map/ppermute | solution.py:817
  335.4 15.6 %collective-permute-start.26 = (bf16[5,24,768]{2,1,0:T(8,128)(2,1)S(1)}, bf16[5,24,768]{2,1,0:T(8,128)(2,1)S(1)}, u32[]{:S(2)}, u32[]{:S(2)}) collective-permute-start(bf16[5,24,768]{2,1,0:T(8,128)(2,1)S(1)} %get-tuple-element.491), channel_id=1, source_target_pairs={{0,4},{2,6},{4,0},{6,2},{1,5},{3,7},{5,1},{7,3},{8,12},{10,14},{12... | collective-permute-start | bytes 552968 | tf_op jit(solution)/shard_map/ppermute | solution.py:817
  336.7 14.3 %collective-permute-start.27 = (bf16[5,24,768]{2,1,0:T(8,128)(2,1)S(1)}, bf16[5,24,768]{2,1,0:T(8,128)(2,1)S(1)}, u32[]{:S(2)}, u32[]{:S(2)}) collective-permute-start(bf16[5,24,768]{2,1,0:T(8,128)(2,1)S(1)} %get-tuple-element.492), channel_id=1, source_target_pairs={{0,6},{2,4},{4,2},{6,0},{1,7},{3,5},{5,3},{7,1},{8,14},{10,12},{12... | collective-permute-start | bytes 552968 | tf_op jit(solution)/shard_map/ppermute | solution.py:817
  356.8 52.2 %all-to-all-start.7 = ((bf16[32,40,768]{2,1,0:T(8,128)(2,1)}), bf16[32,40,768]{2,1,0:T(8,128)(2,1)S(1)}, u32[]{:S(2)}, u32[]{:S(2)}) async-start(bf16[32,40,768]{2,1,0:T(8,128)(2,1)} %bitcast.104), calls=%async_computation.7 | async-start | bytes 3932160 | tf_op jit(solution)/shard_map/all_to_all | solution.py:935
  380.7 39.2 %collective-permute-start.29 = (bf16[4,4,24,768]{3,2,1,0:T(8,128)(2,1)}, bf16[4,4,24,768]{3,2,1,0:T(8,128)(2,1)S(1)}, u32[]{:S(2)}, u32[]{:S(2)}) collective-permute-start(bf16[4,4,24,768]{3,2,1,0:T(8,128)(2,1)} %get-tuple-element.503), channel_id=1, source_target_pairs={{0,1},{1,0},{16,17},{17,16},{2,3},{3,2},{18,19},{19,18},{4,5},{5,4... | collective-permute-start | bytes 1769480 | tf_op jit(solution)/shard_map/ppermute | solution.py:817
  382.6 37.4 %collective-permute-start.30 = (bf16[4,4,24,768]{3,2,1,0:T(8,128)(2,1)}, bf16[4,4,24,768]{3,2,1,0:T(8,128)(2,1)S(1)}, u32[]{:S(2)}, u32[]{:S(2)}) collective-permute-start(bf16[4,4,24,768]{3,2,1,0:T(8,128)(2,1)} %get-tuple-element.504), channel_id=1, source_target_pairs={{0,16},{1,17},{16,0},{17,1},{2,18},{3,19},{18,2},{19,3},{4,20},{5,... | collective-permute-start | bytes 1769480 | tf_op jit(solution)/shard_map/ppermute | solution.py:817
  384.1 35.9 %collective-permute-start.31 = (bf16[4,4,24,768]{3,2,1,0:T(8,128)(2,1)}, bf16[4,4,24,768]{3,2,1,0:T(8,128)(2,1)}, u32[]{:S(2)}, u32[]{:S(2)}) collective-permute-start(bf16[4,4,24,768]{3,2,1,0:T(8,128)(2,1)} %get-tuple-element.505), channel_id=1, source_target_pairs={{0,17},{1,16},{16,1},{17,0},{2,19},{3,18},{18,3},{19,2},{4,21},{5,... | collective-permute-start | bytes 1769480 | tf_op jit(solution)/shard_map/ppermute | solution.py:817
  423.3 13.5 %collective-permute-start.33 = (bf16[4,24,768]{2,1,0:T(8,128)(2,1)S(1)}, bf16[4,24,768]{2,1,0:T(8,128)(2,1)S(1)}, u32[]{:S(2)}, u32[]{:S(2)}) collective-permute-start(bf16[4,24,768]{2,1,0:T(8,128)(2,1)S(1)} %get-tuple-element.521), channel_id=1, source_target_pairs={{0,4},{2,6},{4,0},{6,2},{1,5},{3,7},{5,1},{7,3},{8,12},{10,14},{12... | collective-permute-start | bytes 442376 | tf_op jit(solution)/shard_map/ppermute | solution.py:817
  425.0 11.8 %collective-permute-start.34 = (bf16[4,24,768]{2,1,0:T(8,128)(2,1)S(1)}, bf16[4,24,768]{2,1,0:T(8,128)(2,1)S(1)}, u32[]{:S(2)}, u32[]{:S(2)}) collective-permute-start(bf16[4,24,768]{2,1,0:T(8,128)(2,1)S(1)} %get-tuple-element.522), channel_id=1, source_target_pairs={{0,6},{2,4},{4,2},{6,0},{1,7},{3,5},{5,3},{7,1},{8,14},{10,12},{12... | collective-permute-start | bytes 442376 | tf_op jit(solution)/shard_map/ppermute | solution.py:817
  440.5 12.1 %all-to-all-start.8 = ((f32[32,1,128]{2,1,0:T(1,128)}), f32[32,1,128]{2,1,0:T(1,128)S(1)}, u32[]{:S(2)}, u32[]{:S(2)}) async-start(f32[32,1,128]{2,1,0:T(1,128)} %get-tuple-element.523), calls=%async_computation.8 | async-start | bytes 32768 | tf_op jit(solution)/shard_map/all_to_all | solution.py:1067
  (63 other events, 646.9 us)
Sparse Core Ops, SparseCore 0:
  10.8 49.1 all-gather.1
